TPU v7x, 32 devices: a whole 2x2x4 slice. The times are simulated.
32 devices in a mesh: seq: 16 (over z, y, core), head: 2 (over x).
Axes of the slice: x: 2, y: 2, z: 4, core: 2. Of those that a mesh axis runs over, the one named last changes fastest.
Arguments:
- tokens: bfloat16 [2, 64, 4096], P(None, None, 'seq'), may hold values from -6 to 6
- lengths: int32 [64], replicated, may hold values from 1 to 8192, as said below
- page_owner: int32 [512], P('seq'), may hold values from -1 to 63, as said below
- page_number: int32 [512], P('seq'), may hold values from 0 to 127, as said below
- key_pages: bfloat16 [512, 64, 4096], P('seq', None, 'head'), may hold values from -600 to 600
- value_pages: bfloat16 [512, 64, 4096], P('seq', None, 'head'), may hold values from -6 to 6
- alibi_slopes: float32 [32], P('head'), as said below
- norm1_gain: float32 [4096], P('seq'), may hold values from 0.1 to 1.9
- norm2_gain: float32 [4096], P('seq'), may hold values from 0.1 to 1.9
- w_qkv: bfloat16 [4096, 3, 4096], P('seq', None, 'head'), may hold values from -0.09375 to 0.09375
- w_out: bfloat16 [4096, 4096], P('seq', 'head'), may hold values from -0.09375 to 0.09375
- w_up: bfloat16 [4096, 16384], P('seq', 'head'), may hold values from -0.09375 to 0.09375
- w_down: bfloat16 [4096, 16384], P('seq', 'head'), may hold values from -0.046875 to 0.046875
Outputs:
- layer_out: bfloat16 [2, 64, 4096], P(None, None, 'seq')
Inputs may be any that keep to these rules, and one draw needn't show every extreme that they name: Exactly one request holds 8192 tokens; request r's cache fills page_number 0 .. ceil(lengths[r] / 64) - 1. `page_owner`: -1 marks a free slot; every page of every request stands in exactly one slot; on some indices of seq all 32 slots are used. `page_number`: 0 for free slots. `alibi_slopes`: Positive.
All inputs are finite; a program needn't handle non-finite values.
Results may differ from a plain program's by a relative error of at most 0.011.
Values may be sent and summed in bfloat16 or wider, within the bound.
A program may use at most 128 MiB of HBM per device.

v0:
```python
import jax
import jax.numpy as jnp
from jax import lax
from jax.sharding import PartitionSpec as P

D = 4096
BLK = 8


eps_norm = 1e-05
floor_score = -1e30
highest = lax.Precision.HIGHEST


def normalize(token_rows, gain_share, totals, width_all):
    row_sum, row_squares = totals
    mean_value = row_sum / width_all
    variance = row_squares / width_all - mean_value * mean_value
    return (
        (token_rows.astype(jnp.float32) - mean_value[:, None])
        * lax.rsqrt(variance + eps_norm)[:, None]
        * gain_share[None, :]
    ).astype(jnp.bfloat16)


def page_block(
    carry_state, owners, number, key_block, value_block, queries, slopes, lengths, token_step
):
    run_max, run_sum, run_out = carry_state
    nblock, page_len, width_all = key_block.shape
    nheads = slopes.shape[0]
    head_size = width_all // nheads
    requests = queries.shape[0]
    safe_owner = jnp.clip(owners, 0, requests - 1)
    page_query = jnp.take(queries, safe_owner, axis=0)
    key_heads = key_block.reshape(nblock, page_len, nheads, head_size)
    value_heads = value_block.reshape(nblock, page_len, nheads, head_size)
    scores = jnp.einsum(
        "bhe,bthe->bth", page_query, key_heads, preferred_element_type=jnp.float32
    ) * head_size ** (-0.5)
    positions = number[:, None] * page_len + jnp.arange(page_len, dtype=jnp.int32)[None, :]
    own_length = jnp.take(lengths, safe_owner)
    distance = (own_length[:, None] + token_step - positions).astype(jnp.float32)
    scores = scores - distance[:, :, None] * slopes[None, None, :]
    valid_mask = (owners[:, None] >= 0) & (positions < own_length[:, None])
    masked = jnp.where(valid_mask[:, :, None], scores, floor_score)
    page_max = jnp.max(masked, axis=1)
    member = owners[None, :] == jnp.arange(requests, dtype=jnp.int32)[:, None]
    block_max = jnp.max(jnp.where(member[:, :, None], page_max[None, :, :], floor_score), axis=1)
    next_max = jnp.maximum(run_max, block_max)
    owner_max = jnp.take(next_max, safe_owner, axis=0)
    expon = jnp.where(valid_mask[:, :, None], jnp.exp(masked - owner_max[:, None, :]), 0.0)
    page_sum = jnp.sum(expon, axis=1)
    weights = expon.astype(jnp.bfloat16)
    page_out = jnp.einsum("bth,bthe->bhe", weights, value_heads, preferred_element_type=jnp.float32)
    member_float = member.astype(jnp.float32)
    rescale = jnp.exp(run_max - next_max)
    next_sum = run_sum * rescale + jnp.dot(member_float, page_sum, precision=highest)
    added = jnp.dot(member_float, page_out.reshape(nblock, nheads * head_size), precision=highest)
    next_out = run_out * rescale[:, :, None] + added.reshape(requests, nheads, head_size)
    return (next_max, next_sum, next_out)


def attend_new(carry_state, queries, new_keys, new_values, slopes, token_step):
    run_max, run_sum, run_out = carry_state
    head_size = queries.shape[2]
    for earlier in range(token_step + 1):
        scores = jnp.sum(
            queries.astype(jnp.float32) * new_keys[earlier].astype(jnp.float32), axis=2
        ) * head_size ** (-0.5)
        scores = scores - slopes[None, :] * float(token_step - earlier)
        next_max = jnp.maximum(run_max, scores)
        rescale = jnp.exp(run_max - next_max)
        expon = jnp.exp(scores - next_max)
        weights = lax.optimization_barrier(expon.astype(jnp.bfloat16)).astype(jnp.float32)
        run_sum = run_sum * rescale + expon
        run_out = run_out * rescale[:, :, None] + weights[:, :, None] * new_values[earlier].astype(
            jnp.float32
        )
        run_max = next_max
    attended = (run_out / run_sum[:, :, None]).astype(jnp.bfloat16)
    return attended.reshape(attended.shape[0], -1)


def on_device(
    tokens,
    lengths,
    page_owner,
    page_number,
    key_pages,
    value_pages,
    alibi_slopes,
    norm1_gain,
    norm2_gain,
    w_qkv,
    w_out,
    w_up,
    w_down,
):
    nsteps, requests, local_width = tokens.shape
    nheads = alibi_slopes.shape[0]
    head_width = key_pages.shape[2]
    head_size = head_width // nheads
    nblocks = key_pages.shape[0] // BLK
    qkv_width = w_qkv.shape[1] * w_qkv.shape[2]
    new_keys = []
    new_values = []
    outputs = []
    for token_step in range(nsteps):
        token_rows = tokens[token_step]
        token_float = token_rows.astype(jnp.float32)
        totals = lax.psum(
            (jnp.sum(token_float, axis=1), jnp.sum(token_float * token_float, axis=1)), "seq"
        )
        normed = normalize(token_rows, norm1_gain, totals, D)
        partial_qkv = jnp.dot(
            normed, w_qkv.reshape(local_width, qkv_width), preferred_element_type=jnp.float32
        )
        joined = lax.psum(partial_qkv, "seq").astype(jnp.bfloat16)
        queries = joined[:, :head_width].reshape(requests, nheads, head_size)
        new_keys.append(joined[:, head_width : 2 * head_width].reshape(requests, nheads, head_size))
        new_values.append(joined[:, 2 * head_width :].reshape(requests, nheads, head_size))
        carry_state = (
            jnp.full((requests, nheads), floor_score, jnp.float32),
            jnp.zeros((requests, nheads), jnp.float32),
            jnp.zeros((requests, nheads, head_size), jnp.float32),
        )

        def visit(turn_index, state_in):
            first_page = (turn_index * BLK).astype(jnp.int32)
            owners = lax.dynamic_slice_in_dim(page_owner, first_page, BLK, 0)
            number = lax.dynamic_slice_in_dim(page_number, first_page, BLK, 0)
            key_block = lax.dynamic_slice_in_dim(key_pages, first_page, BLK, 0)
            value_block = lax.dynamic_slice_in_dim(value_pages, first_page, BLK, 0)

            def compute(state_given):
                return page_block(
                    state_given,
                    owners,
                    number,
                    key_block,
                    value_block,
                    queries,
                    alibi_slopes,
                    lengths,
                    token_step,
                )

            def keep_state(state_given):
                return state_given

            return lax.cond(jnp.any(owners >= 0), compute, keep_state, state_in)

        carry_state = lax.fori_loop(0, nblocks, visit, carry_state)
        run_max, run_sum, run_out = carry_state
        top_max = lax.pmax(run_max, "seq")
        rescale = jnp.exp(run_max - top_max)
        run_sum, run_out = lax.psum((run_sum * rescale, run_out * rescale[:, :, None]), "seq")
        run_max = top_max
        attended = attend_new(
            (run_max, run_sum, run_out), queries, new_keys, new_values, alibi_slopes, token_step
        )
        projected = lax.psum(
            lax.dot_general(
                attended, w_out, (((1,), (1,)), ((), ())), preferred_element_type=jnp.float32
            ),
            "head",
        )
        hidden_in = (token_float + projected).astype(jnp.bfloat16)
        hidden_float = hidden_in.astype(jnp.float32)
        totals_two = lax.psum(
            (jnp.sum(hidden_float, axis=1), jnp.sum(hidden_float * hidden_float, axis=1)), "seq"
        )
        normed_two = normalize(hidden_in, norm2_gain, totals_two, D)
        up_proj = jnp.dot(normed_two, w_up, preferred_element_type=jnp.float32)
        up_share = lax.psum_scatter(up_proj, "seq", scatter_dimension=1, tiled=True)
        hidden_share = jax.nn.gelu(up_share, approximate=False).astype(jnp.bfloat16)
        down_part = lax.dot_general(
            lax.all_gather(hidden_share, "seq", axis=1, tiled=True),
            w_down,
            (((1,), (1,)), ((), ())),
            preferred_element_type=jnp.float32,
        )
        down_proj = lax.psum(down_part, "head")
        outputs.append((hidden_float + down_proj).astype(jnp.bfloat16))
    return jnp.stack(outputs)


def solution(mesh):
    placed = (
        P(None, None, "seq"),
        P(),
        P("seq"),
        P("seq"),
        P("seq", None, "head"),
        P("seq", None, "head"),
        P("head"),
        P("seq"),
        P("seq"),
        P("seq", None, "head"),
        P("seq", "head"),
        P("seq", "head"),
        P("seq", "head"),
    )
    return jax.shard_map(
        on_device, mesh=mesh, in_specs=placed, out_specs=P(None, None, "seq"), check_vma=False
    )
```

profile of v0, /device:TPU:31, one launch (start us, length us, event | category | flops | bytes accessed | tf_op | source)
XLA Modules:
  0.0 738.3 jit_solution(16022927175006945250)
XLA Ops:
  8.4 4.7 copy.83
  13.2 28.9 %all-reduce.3 = (f32[64]{0:T(128)S(1)}, f32[64]{0:T(128)S(1)}, f32[64]{0:T(128)S(1)}, f32[64]{0:T(128)S(1)}) all-reduce(f32[64]{0:T(128)S(1)} %get-tuple-element.600, f32[64]{0:T(128)S(1)} %get-tuple-element.598, f32[64]{0:T(128)S(1)} %get-tuple-element.599, f32[64]{0:T(128)S(1)} %get-tuple-element.597), channel_id=1, replica_groups=mesh['seq'=16,'head'=2] {'seq'}, use_global_device_ids=true, to_apply=%region_27.31 | all-reduce | flops 256 | bytes 2048 | tf_op jit(solution)/shard_map/psum | solution.py:112
  42.1 3.1 fusion.107
  45.2 2.2 fusion.110
  47.5 79.6 %all-reduce.18 = (bf16[64,6144]{1,0:T(8,128)(2,1)}, bf16[64,6144]{1,0:T(8,128)(2,1)S(1)}) all-reduce(f32[64,6144]{1,0:T(8,128)S(1)} %fusion.107, f32[64,6144]{1,0:T(8,128)} %fusion.110), channel_id=1, replica_groups=mesh['seq'=16,'head'=2] {'seq'}, use_global_device_ids=true, to_apply=%region_28.32 | all-reduce | flops 786432 | bytes 4718592 | tf_op jit(solution)/shard_map/psum | solution.py:119
  131.8 75.7 %while.35 = (s32[]{:T(128)}, f32[64,16]{0,1:T(8,128)S(1)}, f32[64,16]{0,1:T(8,128)}, f32[64,16,128]{2,0,1:T(8,128)}, s32[32]{0:T(128)}, /*index=5*/s32[32]{0:T(1...) while((s32[]{:T(128)}, f32[64,16]{0,1:T(8,128)S(1)}, ...), condition=%wide.region_36.40_spmd, body=%wide.region_29.39_spmd.sunk | while | flops 17285636 | bytes 14121509 | solution.py:154
  133.8 16.9 %conditional.5 = ((f32[64,16]{0,1:T(8,128)S(1)}, f32[64,16]{0,1:T(8,128)}, f32[64,16,128]{2,0,1:T(8,128)})) conditional(s32[]{:T(128)} %convert_element_type.340, (f32[64,16]{0,1:T(8,128)S(1)}, f32[64,16]{0,1:T(8,128)}, f32[64,16,128]{2,0,1:T(8,128)}) %tuple.134, (s32[8]{0:T(128)S(1)}, s32[32]{0:T(128)}, s32[]{:T(128)}, s32[64]{0:T(128)S(1)}, ...), branch_computations={%region_31.34_spmd, %region_32.38_spmd} | conditional | flops 17285616 | bytes 14121128 | solution.py:152
  133.9 4.0 dynamic-slice_bitcast_fusion.2
  140.0 2.8 fusion.22
  146.2 1.5 convolution_add_fusion.3
  148.4 2.4 convolution_add_fusion.2
  152.8 16.9 %conditional.5 = ((f32[64,16]{0,1:T(8,128)S(1)}, f32[64,16]{0,1:T(8,128)}, f32[64,16,128]{2,0,1:T(8,128)})) conditional(s32[]{:T(128)} %convert_element_type.340, (f32[64,16]{0,1:T(8,128)S(1)}, f32[64,16]{0,1:T(8,128)}, f32[64,16,128]{2,0,1:T(8,128)}) %tuple.134, (s32[8]{0:T(128)S(1)}, s32[32]{0:T(128)}, s32[]{:T(128)}, s32[64]{0:T(128)S(1)}, ...), branch_computations={%region_31.34_spmd, %region_32.38_spmd} | conditional | flops 17285616 | bytes 14121128 | solution.py:152
  152.8 4.0 dynamic-slice_bitcast_fusion.2
  158.9 2.8 fusion.22
  165.1 1.5 convolution_add_fusion.3
  167.3 2.4 convolution_add_fusion.2
  171.7 16.9 %conditional.5 = ((f32[64,16]{0,1:T(8,128)S(1)}, f32[64,16]{0,1:T(8,128)}, f32[64,16,128]{2,0,1:T(8,128)})) conditional(s32[]{:T(128)} %convert_element_type.340, (f32[64,16]{0,1:T(8,128)S(1)}, f32[64,16]{0,1:T(8,128)}, f32[64,16,128]{2,0,1:T(8,128)}) %tuple.134, (s32[8]{0:T(128)S(1)}, s32[32]{0:T(128)}, s32[]{:T(128)}, s32[64]{0:T(128)S(1)}, ...), branch_computations={%region_31.34_spmd, %region_32.38_spmd} | conditional | flops 17285616 | bytes 14121128 | solution.py:152
  171.7 4.0 dynamic-slice_bitcast_fusion.2
  177.9 2.8 fusion.22
  186.2 2.4 convolution_add_fusion.2
  190.6 16.9 %conditional.5 = ((f32[64,16]{0,1:T(8,128)S(1)}, f32[64,16]{0,1:T(8,128)}, f32[64,16,128]{2,0,1:T(8,128)})) conditional(s32[]{:T(128)} %convert_element_type.340, (f32[64,16]{0,1:T(8,128)S(1)}, f32[64,16]{0,1:T(8,128)}, f32[64,16,128]{2,0,1:T(8,128)}) %tuple.134, (s32[8]{0:T(128)S(1)}, s32[32]{0:T(128)}, s32[]{:T(128)}, s32[64]{0:T(128)S(1)}, ...), branch_computations={%region_31.34_spmd, %region_32.38_spmd} | conditional | flops 17285616 | bytes 14121128 | solution.py:152
  190.6 4.0 dynamic-slice_bitcast_fusion.2
  196.8 2.8 fusion.22
  205.1 2.4 convolution_add_fusion.2
  209.0 74.9 %while.34 = (s32[]{:T(128)}, f32[64,16]{0,1:T(8,128)S(1)}, f32[64,16]{0,1:T(8,128)}, f32[64,16,128]{2,0,1:T(8,128)}, s32[32]{0:T(128)}, /*index=5*/s32[32]{0:T(1...) while((s32[]{:T(128)}, f32[64,16]{0,1:T(8,128)S(1)}, ...), condition=%wide.region_12.16_spmd, body=%wide.region_5.15_spmd.sunk | while | flops 17285628 | bytes 14121537 | solution.py:154
  211.1 16.6 %conditional.4 = ((f32[64,16]{0,1:T(8,128)S(1)}, f32[64,16]{0,1:T(8,128)}, f32[64,16,128]{2,0,1:T(8,128)})) conditional(s32[]{:T(128)} %convert_element_type.339, (f32[64,16]{0,1:T(8,128)S(1)}, f32[64,16]{0,1:T(8,128)}, f32[64,16,128]{2,0,1:T(8,128)}) %tuple.130, (s32[8]{0:T(128)S(1)}, s32[32]{0:T(128)}, s32[]{:T(128)}, s32[64]{0:T(128)S(1)}, ...), branch_computations={%region_7.0_spmd, %region_8.14_spmd} | conditional | flops 17285608 | bytes 14121156 | solution.py:152
  211.1 4.0 dynamic-slice_bitcast_fusion
  216.3 2.8 fusion.3
  223.2 1.5 convolution_add_fusion.1
  225.3 2.4 convolution_add_fusion
  229.8 16.6 %conditional.4 = ((f32[64,16]{0,1:T(8,128)S(1)}, f32[64,16]{0,1:T(8,128)}, f32[64,16,128]{2,0,1:T(8,128)})) conditional(s32[]{:T(128)} %convert_element_type.339, (f32[64,16]{0,1:T(8,128)S(1)}, f32[64,16]{0,1:T(8,128)}, f32[64,16,128]{2,0,1:T(8,128)}) %tuple.130, (s32[8]{0:T(128)S(1)}, s32[32]{0:T(128)}, s32[]{:T(128)}, s32[64]{0:T(128)S(1)}, ...), branch_computations={%region_7.0_spmd, %region_8.14_spmd} | conditional | flops 17285608 | bytes 14121156 | solution.py:152
  229.8 4.0 dynamic-slice_bitcast_fusion
  235.0 2.8 fusion.3
  241.9 1.5 convolution_add_fusion.1
  244.0 2.4 convolution_add_fusion
  248.5 16.6 %conditional.4 = ((f32[64,16]{0,1:T(8,128)S(1)}, f32[64,16]{0,1:T(8,128)}, f32[64,16,128]{2,0,1:T(8,128)})) conditional(s32[]{:T(128)} %convert_element_type.339, (f32[64,16]{0,1:T(8,128)S(1)}, f32[64,16]{0,1:T(8,128)}, f32[64,16,128]{2,0,1:T(8,128)}) %tuple.130, (s32[8]{0:T(128)S(1)}, s32[32]{0:T(128)}, s32[]{:T(128)}, s32[64]{0:T(128)S(1)}, ...), branch_computations={%region_7.0_spmd, %region_8.14_spmd} | conditional | flops 17285608 | bytes 14121156 | solution.py:152
  248.6 4.0 dynamic-slice_bitcast_fusion
  253.8 2.8 fusion.3
  260.6 1.5 convolution_add_fusion.1
  262.8 2.4 convolution_add_fusion
  267.3 16.6 %conditional.4 = ((f32[64,16]{0,1:T(8,128)S(1)}, f32[64,16]{0,1:T(8,128)}, f32[64,16,128]{2,0,1:T(8,128)})) conditional(s32[]{:T(128)} %convert_element_type.339, (f32[64,16]{0,1:T(8,128)S(1)}, f32[64,16]{0,1:T(8,128)}, f32[64,16,128]{2,0,1:T(8,128)}) %tuple.130, (s32[8]{0:T(128)S(1)}, s32[32]{0:T(128)}, s32[]{:T(128)}, s32[64]{0:T(128)S(1)}, ...), branch_computations={%region_7.0_spmd, %region_8.14_spmd} | conditional | flops 17285608 | bytes 14121156 | solution.py:152
  267.3 4.0 dynamic-slice_bitcast_fusion
  272.5 2.8 fusion.3
  279.3 1.5 convolution_add_fusion.1
  281.5 2.3 convolution_add_fusion
  283.8 57.1 %all-reduce.5 = (f32[64,16]{0,1:T(8,128)S(1)}, f32[64,16]{0,1:T(8,128)S(1)}) all-reduce(f32[64,16]{0,1:T(8,128)S(1)} %get-tuple-element.592, f32[64,16]{0,1:T(8,128)S(1)} %get-tuple-element.589), channel_id=1, replica_groups=mesh['seq'=16,'head'=2] {'seq'}, use_global_device_ids=true, to_apply=%region_37.41 | all-reduce | flops 2048 | bytes 16384 | tf_op jit(solution)/shard_map/pmax | solution.py:156
  343.0 2.1 broadcast_multiply_fusion
  345.1 2.1 broadcast_multiply_fusion.1
  348.9 57.9 %all-reduce.1 = (f32[64,16]{0,1:T(8,128)S(1)}, f32[64,16]{0,1:T(8,128)S(1)}) all-reduce(f32[64,16]{0,1:T(8,128)S(1)} %get-tuple-element.689, f32[64,16]{0,1:T(8,128)} %get-tuple-element.687), channel_id=1, replica_groups=mesh['seq'=16,'head'=2] {'seq'}, use_global_device_ids=true, to_apply=%region_41.45 | all-reduce | flops 2048 | bytes 16384 | tf_op jit(solution)/shard_map/psum | solution.py:158
  406.9 32.7 %all-reduce.13.cloned.1.call-done = (f32[64,16,128]{2,0,1:T(8,128)}, f32[64,16,128]{2,0,1:T(8,128)}) async-done(((f32[64,16,128]{2,0,1:T(8,128)}, f32[64,16,128]{2,0,1:T(8,128)}), (f32[64,16,128]{2,0,1:T(8,128)}, f32[64,16,128]{2,0,1:T(8,128)})) %all-reduce.13.cloned.1.call-update) | async-done | bytes 1048592 | tf_op jit(solution)/shard_map/psum | solution.py:158
  439.7 2.3 fusion.54
  444.2 22.1 %all-reduce.17.cloned.1.call-done = (f32[64,256]{1,0:T(8,128)}, f32[64,256]{1,0:T(8,128)}) async-done(((f32[64,256]{1,0:T(8,128)}, f32[64,256]{1,0:T(8,128)}), (f32[64,256]{1,0:T(8,128)}, f32[64,256]{1,0:T(8,128)})) %all-reduce.17.cloned.1.call-update) | async-done | bytes 131088 | tf_op jit(solution)/shard_map/psum | solution.py:163
  467.4 29.0 %all-reduce = (f32[64]{0:T(128)S(1)}, f32[64]{0:T(128)S(1)}, f32[64]{0:T(128)S(1)}, f32[64]{0:T(128)S(1)}) all-reduce(f32[64]{0:T(128)S(1)} %get-tuple-element.712, f32[64]{0:T(128)S(1)} %get-tuple-element.713, f32[64]{0:T(128)S(1)} %get-tuple-element.602, f32[64]{0:T(128)S(1)} %get-tuple-element.601), channel_id=1, replica_groups=mesh['seq'=16,'head'=2] {'seq'}, use_global_device_ids=true, to_apply=%region_46.50 | all-reduce | flops 256 | bytes 2048 | tf_op jit(solution)/shard_map/psum | solution.py:171
  496.4 4.4 fusion.101
  500.8 4.4 fusion.104
  505.5 54.6 %reduce-scatter.5.cloned.1.call-done = f32[64,512]{1,0:T(8,128)} async-done(((f32[64,8192]{1,0:T(8,128)}), f32[64,512]{1,0:T(8,128)}) %reduce-scatter.5.cloned.1.call-update) | async-done | bytes 131088 | tf_op jit(solution)/shard_map/reduce_scatter | solution.py:176
  560.2 1.8 fusion.61
  562.1 62.7 %reduce-scatter.3.cloned.1.call-done = f32[64,512]{1,0:T(8,128)} async-done(((f32[64,8192]{1,0:T(8,128)}), f32[64,512]{1,0:T(8,128)}) %reduce-scatter.3.cloned.1.call-update) | async-done | bytes 131088 | tf_op jit(solution)/shard_map/reduce_scatter | solution.py:176
  624.8 1.8 fusion.58
  626.6 38.7 %all-gather.5.cloned.1.call-done = bf16[64,8192]{1,0:T(8,128)(2,1)} async-done(((bf16[64,512]{1,0:T(8,128)(2,1)}), bf16[64,8192]{1,0:T(8,128)(2,1)}) %all-gather.5.cloned.1.call-update) | async-done | bytes 1048592 | tf_op jit(solution)/shard_map/all_gather | solution.py:179
  665.3 4.5 fusion.140
  669.9 33.8 %all-gather.3.cloned.1.call-done = bf16[64,8192]{1,0:T(8,128)(2,1)} async-done(((bf16[64,512]{1,0:T(8,128)(2,1)}), bf16[64,8192]{1,0:T(8,128)(2,1)}) %all-gather.3.cloned.1.call-update) | async-done | bytes 1048592 | tf_op jit(solution)/shard_map/all_gather | solution.py:179
  703.7 4.5 fusion.139
  708.3 20.9 %all-reduce.15.cloned.1.call-done = (f32[64,256]{1,0:T(8,128)}, f32[64,256]{1,0:T(8,128)}) async-done(((f32[64,256]{1,0:T(8,128)}, f32[64,256]{1,0:T(8,128)}), (f32[64,256]{1,0:T(8,128)}, f32[64,256]{1,0:T(8,128)})) %all-reduce.15.cloned.1.call-update) | async-done | bytes 131088 | tf_op jit(solution)/shard_map/psum | solution.py:184
  (262 shorter events, 80.3 us)
Async XLA Ops:
  6.5 435.4 %copy-start = (bf16[256,2048]{1,0:T(8,128)(2,1)S(1)}, bf16[256,2048]{1,0:T(8,128)(2,1)}, u32[]{:S(2)}) copy-start(bf16[256,2048]{1,0:T(8,128)(2,1)} %param.37) | copy-start | bytes 3145732
  6.5 433.1 %all-reduce.13.cloned.1.call-start = ((), (), s32[]{:S(2)}) async-start(), calls=%async_computation.6 | async-start | bytes 2097152 | tf_op jit(solution)/shard_map/psum | solution.py:158
  8.4 33.7 %copy-start.8 = (bf16[2,64,256]{2,1,0:T(8,128)(2,1)S(1)}, bf16[2,64,256]{2,1,0:T(8,128)(2,1)}, u32[]{:S(2)}) copy-start(bf16[2,64,256]{2,1,0:T(8,128)(2,1)} %param.27) | copy-start | bytes 196612
  8.4 33.7 %copy-start.17 = (f32[256]{0:T(256)S(1)}, f32[256]{0:T(256)}, u32[]{:S(2)}) copy-start(f32[256]{0:T(256)} %param.34) | copy-start | bytes 3076
  42.1 3.1 copy-start.2
  127.1 1.4 copy-start.10
  128.1 3.7 copy-start.1
  128.1 3.7 copy-start.11
  133.9 11.3 %copy-start.13 = (s32[8]{0:T(128)}, s32[8]{0:T(128)S(1)}, u32[]{:S(2)}) copy-start(s32[8]{0:T(128)S(1)} %get-tuple-element.557) | copy-start | bytes 100 | tf_op jit(solution)/shard_map/while/body/eval_jaxpr/cond
  146.0 2.4 copy-start.14
  152.8 11.3 %copy-start.13 = (s32[8]{0:T(128)}, s32[8]{0:T(128)S(1)}, u32[]{:S(2)}) copy-start(s32[8]{0:T(128)S(1)} %get-tuple-element.557) | copy-start | bytes 100 | tf_op jit(solution)/shard_map/while/body/eval_jaxpr/cond
  164.9 2.4 copy-start.14
  171.7 11.3 %copy-start.13 = (s32[8]{0:T(128)}, s32[8]{0:T(128)S(1)}, u32[]{:S(2)}) copy-start(s32[8]{0:T(128)S(1)} %get-tuple-element.557) | copy-start | bytes 100 | tf_op jit(solution)/shard_map/while/body/eval_jaxpr/cond
  183.8 2.4 copy-start.14
  190.6 11.3 %copy-start.13 = (s32[8]{0:T(128)}, s32[8]{0:T(128)S(1)}, u32[]{:S(2)}) copy-start(s32[8]{0:T(128)S(1)} %get-tuple-element.557) | copy-start | bytes 100 | tf_op jit(solution)/shard_map/while/body/eval_jaxpr/cond
  202.7 2.4 copy-start.14
  211.1 10.3 %copy-start.15 = (s32[8]{0:T(128)}, s32[8]{0:T(128)S(1)}, u32[]{:S(2)}) copy-start(s32[8]{0:T(128)S(1)} %get-tuple-element.531) | copy-start | bytes 100 | tf_op jit(solution)/shard_map/while/body/eval_jaxpr/cond
  215.7 4.8 copy-start.12
  222.2 3.1 copy-start.16
  229.8 10.3 %copy-start.15 = (s32[8]{0:T(128)}, s32[8]{0:T(128)S(1)}, u32[]{:S(2)}) copy-start(s32[8]{0:T(128)S(1)} %get-tuple-element.531) | copy-start | bytes 100 | tf_op jit(solution)/shard_map/while/body/eval_jaxpr/cond
  234.4 4.8 copy-start.12
  241.0 3.1 copy-start.16
  248.6 10.3 %copy-start.15 = (s32[8]{0:T(128)}, s32[8]{0:T(128)S(1)}, u32[]{:S(2)}) copy-start(s32[8]{0:T(128)S(1)} %get-tuple-element.531) | copy-start | bytes 100 | tf_op jit(solution)/shard_map/while/body/eval_jaxpr/cond
  253.1 4.8 copy-start.12
  259.7 3.1 copy-start.16
  267.3 10.3 %copy-start.15 = (s32[8]{0:T(128)}, s32[8]{0:T(128)S(1)}, u32[]{:S(2)}) copy-start(s32[8]{0:T(128)S(1)} %get-tuple-element.531) | copy-start | bytes 100 | tf_op jit(solution)/shard_map/while/body/eval_jaxpr/cond
  271.8 4.8 copy-start.12
  278.4 3.1 copy-start.16
  283.8 63.4 %copy-start.3 = (f32[8,8,16,128]{3,1,2,0:T(8,128)S(1)}, f32[8,8,16,128]{3,1,2,0:T(8,128)}, u32[]{:S(2)}) copy-start(f32[8,8,16,128]{3,1,2,0:T(8,128)} %get-tuple-element.705) | copy-start | bytes 1572868
  342.9 4.4 copy-start.4
  347.1 92.5 %copy-start.5 = (f32[8,16,8,128]{3,2,1,0:T(8,128)S(1)}, f32[8,16,8,128]{3,2,1,0:T(8,128)}, u32[]{:S(2)}) copy-start(f32[8,16,8,128]{3,2,1,0:T(8,128)} %get-tuple-element.704) | copy-start | bytes 1572868
  347.2 92.5 %copy-start.6 = (f32[8,16,8,128]{3,2,1,0:T(8,128)S(1)}, f32[8,16,8,128]{3,2,1,0:T(8,128)}, u32[]{:S(2)}) copy-start(f32[8,16,8,128]{3,2,1,0:T(8,128)} %get-tuple-element.707) | copy-start | bytes 1572868
  347.2 119.2 %all-reduce.17.cloned.1.call-start = ((), (), s32[]{:S(2)}) async-start(), calls=%async_computation.8 | async-start | bytes 262144 | tf_op jit(solution)/shard_map/psum | solution.py:163
  347.2 1.0 copy-start.7
  441.9 24.4 %copy-start.9 = (bf16[2,64,256]{2,1,0:T(8,128)(2,1)S(1)}, bf16[2,64,256]{2,1,0:T(8,128)(2,1)}, u32[]{:S(2)}) copy-start(bf16[2,64,256]{2,1,0:T(8,128)(2,1)} %param.27) | copy-start | bytes 196612
  442.0 54.4 %copy-start.18 = (f32[256]{0:T(256)S(1)}, f32[256]{0:T(256)}, u32[]{:S(2)}) copy-start(f32[256]{0:T(256)} %param.35) | copy-start | bytes 3076
  444.2 116.0 %reduce-scatter.5.cloned.1.call-start = ((), (), s32[]{:S(2)}) async-start(), calls=%async_computation.4 | async-start | bytes 2228224 | tf_op jit(solution)/shard_map/reduce_scatter | solution.py:176
  500.8 124.0 %reduce-scatter.3.cloned.1.call-start = ((), (), s32[]{:S(2)}) async-start(), calls=%async_computation.2 | async-start | bytes 2228224 | tf_op jit(solution)/shard_map/reduce_scatter | solution.py:176
  505.3 160.0 %all-gather.5.cloned.1.call-start = ((), (), s32[]{:S(2)}) async-start(), calls=%async_computation.5 | async-start | bytes 1114112 | tf_op jit(solution)/shard_map/all_gather | solution.py:179
  562.0 141.7 %all-gather.3.cloned.1.call-start = ((), (), s32[]{:S(2)}) async-start(), calls=%async_computation.3 | async-start | bytes 1114112 | tf_op jit(solution)/shard_map/all_gather | solution.py:179
  626.6 102.5 %all-reduce.15.cloned.1.call-start = ((), (), s32[]{:S(2)}) async-start(), calls=%async_computation.7 | async-start | bytes 262144 | tf_op jit(solution)/shard_map/psum | solution.py:184
Sparse Core Ops, SparseCore 0:
  347.3 92.3 all-reduce.12
  444.3 22.0 all-reduce.16
  500.9 59.2 reduce-scatter.4
  564.2 60.4 reduce-scatter.2
  626.8 38.5 all-gather.4
  667.3 36.3 all-gather.2
  708.4 20.6 all-reduce.14
where the time goes:
time: 744 us; the launch traced here: 738 us
  waiting for transfers between devices  266 us (36%)
  blocking collectives  252 us (34%)
  matrix products  83.6 us (11%)
  local copies, waits for them, and re-layouts  60.9 us (8%)
  other arithmetic  55.5 us (7%)
  between operations  13.7 us (2%)
    reduce_scatter x2, waiting for transfers between devices, on_device(): up_share = lax.psum_scatter(up_proj, 'seq', scatter_dimension=1, tiled=True)  117 us
    psum x1, blocking collectives, on_device(): joined = lax.psum(partial_qkv, 'seq').astype(jnp.bfloat16)  79.6 us
    all_gather x2, waiting for transfers between devices, on_device(): lax.all_gather(hidden_share, 'seq', axis=1, tiled=True)  72.5 us
    psum x1, blocking collectives, on_device(): lax.psum((run_sum * rescale, run_out * rescale[:, :, None]), 'seq')  57.9 us
    pmax x1, blocking collectives, on_device(): top_max = lax.pmax(run_max, 'seq')  57.1 us
    psum x1, waiting for transfers between devices, on_device(): lax.psum((run_sum * rescale, run_out * rescale[:, :, None]), 'seq')  32.7 us
    cond x48, local copies, waits for them, and re-layouts  32.3 us
    psum x1, blocking collectives, on_device(): lax.psum((jnp.sum(hidden_float, axis=1), jnp.sum(hidden_float * hidden_fl...  29 us
  transfers between devices with their start and end apart: 7, of which 7 were waited for; matrix products, arithmetic and copies ran while one was open for 2% of the time, Pallas kernels for 0%

commit v1 on v0

--- a/solution.py
+++ b/solution.py
@@ -1,6 +1,10 @@
+import functools
+
 import jax
 import jax.numpy as jnp
 from jax import lax
+from jax.experimental import pallas as pl
+from jax.experimental.pallas import tpu as pltpu
 from jax.sharding import PartitionSpec as P
 
 D = 4096
@@ -185,6 +189,636 @@
         outputs.append((hidden_float + down_proj).astype(jnp.bfloat16))
     return jnp.stack(outputs)
 
+MESH = pl.DeviceIdType.MESH
+NSEQ = 16
+NZ = 4
+CHUNKS = 2
+VMEM_LIMIT = 60 * 1024 * 1024
+
+
+def place():
+    index = lax.axis_index("seq")
+    return index, index // 4, (index // 2) % 2, index % 2
+
+
+def send(src, dst, send_sem, recv_sem, peer, axis="seq"):
+    copy = pltpu.make_async_remote_copy(
+        src_ref=src,
+        dst_ref=dst,
+        send_sem=send_sem,
+        recv_sem=recv_sem,
+        device_id={axis: peer},
+        device_id_type=MESH,
+    )
+    copy.start()
+    return copy
+
+
+def greet_all(with_head):
+    me = lax.axis_index("seq")
+    barrier = pltpu.get_barrier_semaphore()
+    for step in range(1, NSEQ):
+        pl.semaphore_signal(
+            barrier, inc=1, device_id={"seq": (me + step) % NSEQ}, device_id_type=MESH
+        )
+    if with_head:
+        other = 1 - lax.axis_index("head")
+        pl.semaphore_signal(barrier, inc=1, device_id={"head": other}, device_id_type=MESH)
+    pl.semaphore_wait(barrier, NSEQ - 1 + int(with_head))
+
+
+def row_to_column(row):
+    width = row.shape[1]
+    same = lax.broadcasted_iota(jnp.int32, (width, width), 0) == lax.broadcasted_iota(
+        jnp.int32, (width, width), 1
+    )
+    return jnp.sum(jnp.where(same, row, 0.0), axis=1, keepdims=True)
+
+
+def start_stats(values, stats, send_sem, recv_sem):
+    me = lax.axis_index("seq")
+    ones = jnp.ones((8, values.shape[1]), jnp.float32)
+    contract = (((1,), (1,)), ((), ()))
+    stats[me, 0:8, :] = lax.dot_general(
+        ones, values, contract, precision=highest, preferred_element_type=jnp.float32
+    )
+    stats[me, 8:16, :] = lax.dot_general(
+        ones, values * values, contract, precision=highest, preferred_element_type=jnp.float32
+    )
+    return [
+        send(
+            stats.at[me],
+            stats.at[me],
+            send_sem.at[step - 1],
+            recv_sem.at[step - 1],
+            (me + step) % NSEQ,
+        )
+        for step in range(1, NSEQ)
+    ]
+
+
+def finish_stats(copies, stats):
+    for copy in copies:
+        copy.wait_recv()
+    total = stats[0]
+    for source in range(1, NSEQ):
+        total = total + stats[source]
+    mean = total[0:1, :] / D
+    variance = total[8:9, :] / D - mean * mean
+    return row_to_column(mean), row_to_column(lax.rsqrt(variance + eps_norm))
+
+
+def row_chunks(rows):
+    size = rows // CHUNKS
+    return [pl.ds(k * size, size) for k in range(CHUNKS)]
+
+
+def add_into(target, extra):
+    target[...] = (target[...].astype(jnp.float32) + extra[...].astype(jnp.float32)).astype(
+        jnp.bfloat16
+    )
+
+
+def reduce_scatter(parts, from_core, from_y, from_z, send_sem, recv_sem, finish):
+    me, z, y, c = place()
+    chunks = row_chunks(parts.shape[3])
+    copies = []
+    first = []
+    for k, rows in enumerate(chunks):
+        sem = 5 * k
+        first.append(
+            send(
+                parts.at[1 - c, :, :, rows],
+                from_core.at[:, :, rows],
+                send_sem.at[sem],
+                recv_sem.at[sem],
+                me + 1 - 2 * c,
+            )
+        )
+    second = []
+    for k, rows in enumerate(chunks):
+        first[k].wait_recv()
+        for zz in range(NZ):
+            add_into(parts.at[c, 1 - y, zz, rows], from_core.at[1 - y, zz, rows])
+        sem = 5 * k + 1
+        second.append(
+            send(
+                parts.at[c, 1 - y, :, rows],
+                from_y.at[:, rows],
+                send_sem.at[sem],
+                recv_sem.at[sem],
+                me + 2 - 4 * y,
+            )
+        )
+        for zz in range(NZ):
+            add_into(parts.at[c, y, zz, rows], from_core.at[y, zz, rows])
+    third = []
+    for k, rows in enumerate(chunks):
+        second[k].wait_recv()
+        sent = []
+        for step in range(1, NZ):
+            to = (z + step) % NZ
+            add_into(parts.at[c, y, to, rows], from_y.at[to, rows])
+            sem = 5 * k + 1 + step
+            sent.append(
+                send(
+                    parts.at[c, y, to, rows],
+                    from_z.at[step - 1, rows],
+                    send_sem.at[sem],
+                    recv_sem.at[sem],
+                    to * 4 + y * 2 + c,
+                )
+            )
+        third.append(sent)
+    for k, rows in enumerate(chunks):
+        total = parts[c, y, z, rows].astype(jnp.float32) + from_y[z, rows].astype(jnp.float32)
+        for step in range(1, NZ):
+            third[k][step - 1].wait_recv()
+            total = total + from_z[step - 1, rows].astype(jnp.float32)
+        finish(k, rows, total)
+        copies += third[k]
+    return first + second + copies
+
+
+def all_gather(blocks, send_sem, recv_sem):
+    me, z, y, c = place()
+    chunks = row_chunks(blocks.shape[3])
+    first = []
+    for k, rows in enumerate(chunks):
+        own = blocks.at[c, y, z, rows]
+        first.append(
+            [
+                send(
+                    own,
+                    own,
+                    send_sem.at[5 * k + step - 1],
+                    recv_sem.at[5 * k + step - 1],
+                    ((z + step) % NZ) * 4 + y * 2 + c,
+                )
+                for step in range(1, NZ)
+            ]
+        )
+    second = []
+    for k, rows in enumerate(chunks):
+        for copy in first[k]:
+            copy.wait_recv()
+        own = blocks.at[c, y, :, rows]
+        second.append(
+            send(own, own, send_sem.at[5 * k + 3], recv_sem.at[5 * k + 3], me + 2 - 4 * y)
+        )
+    third = []
+    for k, rows in enumerate(chunks):
+        second[k].wait_recv()
+        own = blocks.at[c, :, :, rows]
+        third.append(
+            send(own, own, send_sem.at[5 * k + 4], recv_sem.at[5 * k + 4], me + 1 - 2 * c)
+        )
+    for copy in third:
+        copy.wait_recv()
+    return [copy for group in first for copy in group] + second + third
+
+
+def project_kernel(
+    tokens,
+    gain,
+    w_hbm,
+    q_all,
+    kv_own,
+    w_qkv,
+    stats,
+    parts,
+    from_core,
+    from_y,
+    from_z,
+    stat_send,
+    stat_recv,
+    rs_send,
+    rs_recv,
+    ag_send,
+    ag_recv,
+    load_sem,
+):
+    load = pltpu.make_async_copy(w_hbm, w_qkv, load_sem)
+    load.start()
+    me, z, y, c = place()
+    greet_all(False)
+    token_float = tokens[...].astype(jnp.float32)
+    stat_copies = start_stats(token_float, stats, stat_send, stat_recv)
+    mean, scale = finish_stats(stat_copies, stats)
+    normed = ((token_float - mean) * scale * gain[...]).astype(jnp.bfloat16)
+    load.wait()
+    for head in range(NSEQ):
+        columns = pl.ds(head * 128, 128)
+        for part in range(3):
+            parts[head % 2, (head // 2) % 2, head // 4, :, part * 128 : part * 128 + 128] = jnp.dot(
+                normed, w_qkv[part, :, columns], preferred_element_type=jnp.float32
+            ).astype(jnp.bfloat16)
+
+    def finish(k, rows, total):
+        joined = total.astype(jnp.bfloat16)
+        q_all[c, y, z, rows] = joined[:, :128]
+        kv_own[rows] = joined
+
+    copies = reduce_scatter(parts, from_core, from_y, from_z, rs_send, rs_recv, finish)
+    copies += all_gather(q_all, ag_send, ag_recv)
+    for copy in stat_copies + copies:
+        copy.wait_send()
+
+
+def project(tokens, gain, w_qkv):
+    rows = tokens.shape[0]
+    width = 384
+    vmem = pl.BlockSpec(memory_space=pltpu.VMEM)
+    dma = pltpu.SemaphoreType.DMA
+    bf16 = jnp.bfloat16
+    return pl.pallas_call(
+        project_kernel,
+        out_shape=(
+            jax.ShapeDtypeStruct((2, 2, NZ, rows, 128), bf16),
+            jax.ShapeDtypeStruct((rows, width), bf16),
+        ),
+        in_specs=[vmem, vmem, pl.BlockSpec(memory_space=pl.ANY)],
+        out_specs=(vmem, vmem),
+        scratch_shapes=[
+            pltpu.VMEM(w_qkv.shape, bf16),
+            pltpu.VMEM((NSEQ, 16, rows), jnp.float32),
+            pltpu.VMEM((2, 2, NZ, rows, width), bf16),
+            pltpu.VMEM((2, NZ, rows, width), bf16),
+            pltpu.VMEM((NZ, rows, width), bf16),
+            pltpu.VMEM((NZ - 1, rows, width), bf16),
+            dma((NSEQ - 1,)),
+            dma((NSEQ - 1,)),
+            dma((5 * CHUNKS,)),
+            dma((5 * CHUNKS,)),
+            dma((5 * CHUNKS,)),
+            dma((5 * CHUNKS,)),
+            dma,
+        ],
+        compiler_params=pltpu.CompilerParams(
+            collective_id=0, has_side_effects=True, vmem_limit_bytes=VMEM_LIMIT
+        ),
+        name="project",
+    )(tokens, gain, w_qkv)
+
+
+PAGES_STEP = 8
+
+
+def pages_kernel(owners, numbers, lengths, q_all, slopes, keys, values, out, marks, q_rows):
+    turn = pl.program_id(0)
+    requests = lengths.shape[0]
+    nheads = NSEQ
+    width = nheads * 128
+    page_len = keys.shape[1]
+    root = 128 ** (-0.5)
+
+    @pl.when(turn == 0)
+    def _():
+        for head in range(nheads):
+            q_rows[:, head * 128 : head * 128 + 128] = q_all[
+                head % 2, (head // 2) % 2, head // 4
+            ].astype(jnp.float32)
+        marks[...] = jnp.full_like(marks, -1.0)
+
+    own_head = lax.broadcasted_iota(jnp.int32, (nheads, width), 0) == (
+        lax.broadcasted_iota(jnp.int32, (nheads, width), 1) // 128
+    )
+    slope = jnp.sum(
+        jnp.where(
+            lax.broadcasted_iota(jnp.int32, (nheads, nheads), 0)
+            == lax.broadcasted_iota(jnp.int32, (nheads, nheads), 1),
+            slopes[...],
+            0.0,
+        ),
+        axis=1,
+        keepdims=True,
+    )
+    slope = jnp.concatenate([slope, slope], axis=0)
+    step_row = lax.broadcasted_iota(jnp.int32, (2 * nheads, page_len), 0) // nheads
+    offset = lax.broadcasted_iota(jnp.int32, (2 * nheads, page_len), 1)
+    lane = lax.broadcasted_iota(jnp.int32, (nheads, 128), 1)
+    top_rows = marks[:, 0, :]
+    sum_rows = marks[:, 1, :]
+    owner_rows = marks[:, 2, :]
+    page_outs = []
+    for slot in range(PAGES_STEP):
+        page = turn * PAGES_STEP + slot
+        owner = owners[page]
+        safe = jnp.clip(owner, 0, requests - 1)
+        left = lengths[safe] - numbers[page] * page_len
+        queries = [
+            jnp.where(own_head, q_rows[pl.ds(safe + step * requests, 1), :], 0.0)
+            for step in range(2)
+        ]
+        spread = jnp.concatenate(queries, axis=0).astype(jnp.bfloat16)
+        scores = lax.dot_general(
+            spread, keys[slot], (((1,), (1,)), ((), ())), preferred_element_type=jnp.float32
+        )
+        distance = (left + step_row - offset).astype(jnp.float32)
+        scores = scores * root - distance * slope
+        valid = (offset < left) & (owner >= 0)
+        masked = jnp.where(valid, scores, floor_score)
+        top = jnp.max(masked, axis=1, keepdims=True)
+        expon = jnp.where(valid, jnp.exp(masked - top), 0.0)
+        total = jnp.sum(expon, axis=1, keepdims=True)
+        mixed = jnp.dot(
+            expon.astype(jnp.bfloat16), values[slot], preferred_element_type=jnp.float32
+        )
+        for step in range(2):
+            rows = slice(step * nheads, (step + 1) * nheads)
+            page_outs.append(
+                jnp.sum(jnp.where(own_head, mixed[rows], 0.0), axis=0, keepdims=True)
+            )
+            here = lane == 2 * page + step
+            top_rows = jnp.where(here, top[rows], top_rows)
+            sum_rows = jnp.where(here, total[rows], sum_rows)
+            owner_rows = jnp.where(here, owner.astype(jnp.float32), owner_rows)
+    marks[:, 0, :] = top_rows
+    marks[:, 1, :] = sum_rows
+    marks[:, 2, :] = owner_rows
+    stacked = jnp.concatenate(page_outs, axis=0).astype(jnp.bfloat16)
+    first = pl.multiple_of(turn * 2 * PAGES_STEP, 2 * PAGES_STEP)
+    for head in range(nheads):
+        out[head, pl.ds(first, 2 * PAGES_STEP), :] = stacked[:, head * 128 : head * 128 + 128]
+
+
+def attend_pages(page_owner, page_number, lengths, q_all, slopes, key_pages, value_pages):
+    npages, page_len, width = key_pages.shape
+    rows = q_all.shape[3]
+    block = pl.BlockSpec((PAGES_STEP, page_len, width), lambda i, *_: (i, 0, 0))
+    return pl.pallas_call(
+        pages_kernel,
+        grid_spec=pltpu.PrefetchScalarGridSpec(
+            num_scalar_prefetch=3,
+            grid=(npages // PAGES_STEP,),
+            in_specs=[
+                pl.BlockSpec(q_all.shape, lambda i, *_: (0, 0, 0, 0, 0)),
+                pl.BlockSpec(slopes.shape, lambda i, *_: (0, 0)),
+                block,
+                block,
+            ],
+            out_specs=(
+                pl.BlockSpec((NSEQ, 2 * npages, 128), lambda i, *_: (0, 0, 0)),
+                pl.BlockSpec((NSEQ, 8, 128), lambda i, *_: (0, 0, 0)),
+            ),
+            scratch_shapes=[pltpu.VMEM((rows, width), jnp.float32)],
+        ),
+        out_shape=(
+            jax.ShapeDtypeStruct((NSEQ, 2 * npages, 128), jnp.bfloat16),
+            jax.ShapeDtypeStruct((NSEQ, 8, 128), jnp.float32),
+        ),
+        compiler_params=pltpu.CompilerParams(
+            vmem_limit_bytes=VMEM_LIMIT, dimension_semantics=("arbitrary",)
+        ),
+        name="attend_pages",
+    )(page_owner, page_number, lengths, q_all, slopes, key_pages, value_pages)
+
+
+def combine(qkv, slopes, page_out, marks):
+    rows = qkv.shape[0]
+    requests = rows // 2
+    me = lax.axis_index("seq")
+    joined = qkv[...].astype(jnp.float32)
+    query, new_key, new_value = joined[:, :128], joined[:, 128:256], joined[:, 256:]
+    slope = jnp.sum(
+        jnp.where(lax.broadcasted_iota(jnp.int32, slopes.shape, 1) == me, slopes[...], 0.0),
+        axis=1,
+        keepdims=True,
+    )
+    root = 128 ** (-0.5)
+    same = jnp.sum(query * new_key, axis=1, keepdims=True) * root
+    key_before = jnp.concatenate([new_key[:requests], new_key[:requests]], axis=0)
+    value_before = jnp.concatenate([new_value[:requests], new_value[:requests]], axis=0)
+    later = lax.broadcasted_iota(jnp.int32, (rows, 1), 0) >= requests
+    before = jnp.where(
+        later, jnp.sum(query * key_before, axis=1, keepdims=True) * root - slope, floor_score
+    )
+    row_id = lax.broadcasted_iota(jnp.int32, (rows, 128), 0)
+    lane_step = lax.broadcasted_iota(jnp.int32, (rows, 128), 1) % 2
+    row_step = row_id // requests
+    row_owner = (row_id % requests).astype(jnp.float32)
+
+    def member(source):
+        return (marks[source, 2:3, :] == row_owner) & (lane_step == row_step)
+
+    best = jnp.full((rows, 128), floor_score, jnp.float32)
+    for source in range(NSEQ):
+        best = jnp.maximum(best, jnp.where(member(source), marks[source, 0:1, :], floor_score))
+    top = jnp.maximum(jnp.max(best, axis=1, keepdims=True), jnp.maximum(same, before))
+    e_same = jnp.exp(same - top)
+    e_before = jnp.where(later, jnp.exp(before - top), 0.0)
+    sums = jnp.zeros((rows, 128), jnp.float32)
+    mixed = e_same.astype(jnp.bfloat16).astype(jnp.float32) * new_value + e_before.astype(
+        jnp.bfloat16
+    ).astype(jnp.float32) * value_before
+    live = page_out.shape[1]
+    for source in range(NSEQ):
+        factor = jnp.where(member(source), jnp.exp(marks[source, 0:1, :] - top), 0.0)
+        sums = sums + factor * marks[source, 1:2, :]
+        mixed = mixed + jnp.dot(
+            factor[:, :live].astype(jnp.bfloat16),
+            page_out[source],
+            preferred_element_type=jnp.float32,
+        )
+    total = jnp.sum(sums, axis=1, keepdims=True) + e_same + e_before
+    return (mixed / total).astype(jnp.bfloat16)
+
+
+def finish_kernel(
+    tokens,
+    qkv,
+    slopes,
+    gain,
+    page_out,
+    marks,
+    w_out_hbm,
+    w_up_hbm,
+    w_down_hbm,
+    result,
+    w_out,
+    w_up,
+    w_down,
+    got_out,
+    got_marks,
+    attended,
+    pair_out,
+    stats,
+    parts,
+    from_core,
+    from_y,
+    from_z,
+    hidden,
+    ex_send,
+    ex_recv,
+    pair_send,
+    pair_recv,
+    stat_send,
+    stat_recv,
+    rs_send,
+    rs_recv,
+    ag_send,
+    ag_recv,
+    load_sem,
+):
+    loads = [
+        pltpu.make_async_copy(src, dst, load_sem.at[n])
+        for n, (src, dst) in enumerate(
+            ((w_out_hbm, w_out), (w_up_hbm, w_up), (w_down_hbm, w_down))
+        )
+    ]
+    for load in loads:
+        load.start()
+    me, z, y, c = place()
+    other = 1 - lax.axis_index("head")
+    greet_all(True)
+    copies = []
+    for step in range(1, NSEQ):
+        to = (me + step) % NSEQ
+        n = 2 * (step - 1)
+        copies.append(
+            send(page_out.at[to], got_out.at[me], ex_send.at[n], ex_recv.at[n], to)
+        )
+        copies.append(
+            send(marks.at[to], got_marks.at[me], ex_send.at[n + 1], ex_recv.at[n + 1], to)
+        )
+    got_out[me] = page_out[me]
+    got_marks[me] = marks[me]
+    for copy in copies:
+        copy.wait_recv()
+    attended[c, y, z] = combine(qkv, slopes, got_out, got_marks)
+    copies += all_gather(attended, ag_send.at[0], ag_recv.at[0])
+    contract = (((1,), (1,)), ((), ()))
+    loads[0].wait()
+    projected = jnp.zeros(pair_out.shape[2:], jnp.float32)
+    for head in range(NSEQ):
+        projected = projected + lax.dot_general(
+            attended[head % 2, (head // 2) % 2, head // 4],
+            w_out[:, head * 128 : head * 128 + 128],
+            contract,
+            preferred_element_type=jnp.float32,
+        )
+    pair_out[0, 0] = projected
+    pair = send(
+        pair_out.at[0, 0], pair_out.at[0, 1], pair_send.at[0], pair_recv.at[0], other, "head"
+    )
+    copies.append(pair)
+    pair.wait_recv()
+    hidden_in = (
+        tokens[...].astype(jnp.float32) + (projected + pair_out[0, 1])
+    ).astype(jnp.bfloat16)
+    hidden_float = hidden_in.astype(jnp.float32)
+    stat_copies = start_stats(hidden_float, stats, stat_send, stat_recv)
+    copies += stat_copies
+    mean, scale = finish_stats(stat_copies, stats)
+    normed = ((hidden_float - mean) * scale * gain[...]).astype(jnp.bfloat16)
+    loads[1].wait()
+    share = parts.shape[4]
+    for block in range(NSEQ):
+        parts[block % 2, (block // 2) % 2, block // 4] = jnp.dot(
+            normed,
+            w_up[:, block * share : (block + 1) * share],
+            preferred_element_type=jnp.float32,
+        ).astype(jnp.bfloat16)
+
+    def finish(k, rows, total):
+        hidden[c, y, z, rows] = (0.5 * total * (1.0 + lax.erf(total * 0.5**0.5))).astype(
+            jnp.bfloat16
+        )
+
+    copies += reduce_scatter(parts, from_core, from_y, from_z, rs_send, rs_recv, finish)
+    copies += all_gather(hidden, ag_send.at[1], ag_recv.at[1])
+    loads[2].wait()
+    down = jnp.zeros(pair_out.shape[2:], jnp.float32)
+    for block in range(NSEQ):
+        down = down + lax.dot_general(
+            hidden[block % 2, (block // 2) % 2, block // 4],
+            w_down[:, block * share : (block + 1) * share],
+            contract,
+            preferred_element_type=jnp.float32,
+        )
+    pair_out[1, 0] = down
+    pair = send(
+        pair_out.at[1, 0], pair_out.at[1, 1], pair_send.at[1], pair_recv.at[1], other, "head"
+    )
+    copies.append(pair)
+    pair.wait_recv()
+    result[...] = (hidden_float + (down + pair_out[1, 1])).astype(jnp.bfloat16)
+    for copy in copies:
+        copy.wait_send()
+
+
+def finish_layer(tokens, qkv, slopes, gain, page_out, marks, w_out, w_up, w_down):
+    rows, local_width = tokens.shape
+    share = w_up.shape[1] // NSEQ
+    vmem = pl.BlockSpec(memory_space=pltpu.VMEM)
+    hbm = pl.BlockSpec(memory_space=pl.ANY)
+    dma = pltpu.SemaphoreType.DMA
+    bf16 = jnp.bfloat16
+    return pl.pallas_call(
+        finish_kernel,
+        out_shape=jax.ShapeDtypeStruct((rows, local_width), bf16),
+        in_specs=[vmem] * 6 + [hbm] * 3,
+        out_specs=vmem,
+        scratch_shapes=[
+            pltpu.VMEM(w_out.shape, bf16),
+            pltpu.VMEM(w_up.shape, bf16),
+            pltpu.VMEM(w_down.shape, bf16),
+            pltpu.VMEM(page_out.shape, bf16),
+            pltpu.VMEM(marks.shape, jnp.float32),
+            pltpu.VMEM((2, 2, NZ, rows, 128), bf16),
+            pltpu.VMEM((2, 2, rows, local_width), jnp.float32),
+            pltpu.VMEM((NSEQ, 16, rows), jnp.float32),
+            pltpu.VMEM((2, 2, NZ, rows, share), bf16),
+            pltpu.VMEM((2, NZ, rows, share), bf16),
+            pltpu.VMEM((NZ, rows, share), bf16),
+            pltpu.VMEM((NZ - 1, rows, share), bf16),
+            pltpu.VMEM((2, 2, NZ, rows, share), bf16),
+            dma((2 * NSEQ - 2,)),
+            dma((2 * NSEQ - 2,)),
+            dma((2,)),
+            dma((2,)),
+            dma((NSEQ - 1,)),
+            dma((NSEQ - 1,)),
+            dma((5 * CHUNKS,)),
+            dma((5 * CHUNKS,)),
+            dma((2, 5 * CHUNKS)),
+            dma((2, 5 * CHUNKS)),
+            dma((3,)),
+        ],
+        compiler_params=pltpu.CompilerParams(
+            collective_id=1, has_side_effects=True, vmem_limit_bytes=VMEM_LIMIT
+        ),
+        name="finish_layer",
+    )(tokens, qkv, slopes, gain, page_out, marks, w_out, w_up, w_down)
+
+
+def on_device_kernels(
+    tokens,
+    lengths,
+    page_owner,
+    page_number,
+    key_pages,
+    value_pages,
+    alibi_slopes,
+    norm1_gain,
+    norm2_gain,
+    w_qkv,
+    w_out,
+    w_up,
+    w_down,
+):
+    nsteps, requests, local_width = tokens.shape
+    rows = tokens.reshape(nsteps * requests, local_width)
+    slopes = alibi_slopes[None, :]
+    q_all, qkv = project(rows, norm1_gain[None, :], jnp.transpose(w_qkv, (1, 0, 2)))
+    page_out, marks = attend_pages(
+        page_owner, page_number, lengths, q_all, slopes, key_pages, value_pages
+    )
+    result = finish_layer(
+        rows, qkv, slopes, norm2_gain[None, :], page_out, marks, w_out, w_up, w_down
+    )
+    return result.reshape(tokens.shape)
+
 
 def solution(mesh):
     placed = (
@@ -202,6 +836,7 @@
         P("seq", "head"),
         P("seq", "head"),
     )
+    fits = mesh.shape["seq"] == NSEQ and mesh.shape["head"] == 2
     return jax.shard_map(
-        on_device, mesh=mesh, in_specs=placed, out_specs=P(None, None, "seq"), check_vma=False
-    )
+        on_device_kernels if fits else on_device, mesh=mesh, in_specs=placed, out_specs=P(None, None, "seq"), check_vma=False
+    )

time: 744 us -> 145 us (0.19)
  waiting for transfers between devices: 266 us -> 0 us
  blocking collectives: 252 us -> 0 us
  Pallas kernels: 0 us -> 144 us
  matrix products: 83.6 us -> 0 us
  local copies, waits for them, and re-layouts: 60.9 us -> 1.47 us
  other arithmetic: 55.5 us -> 0 us
  between operations: 13.7 us -> 0.02 us
    psum x4 -> x0, blocking collectives: 195 us -> none  [the longest x1 79.6 us: on_device(): joined = lax.psum(partial_qkv, 'seq').astype(jnp.bfloat16)]
    pallas_call x0 -> x3, Pallas kernels: none -> 144 us  [the longest x1 87.9 us: finish_layer(): pl.pallas_call(finish_kernel, out_shape=jax.ShapeDtypeStruct((rows, local...]
    reduce_scatter x2 -> x0, waiting for transfers between devices: 117 us -> none  [on_device(): up_share = lax.psum_scatter(up_proj, 'seq', scatter_dimension=1, tiled=True)]
    dot_general x40 -> x0, matrix products: 83.6 us -> none  [the longest x8 22.1 us: page_block(): jnp.einsum('bhe,bthe->bth', page_query, key_heads, preferred_element_type...]
    psum x3 -> x0, waiting for transfers between devices: 75.7 us -> none  [the longest x1 32.7 us: on_device(): lax.psum((run_sum * rescale, run_out * rescale[:, :, None]), 'seq')]
    all_gather x2 -> x0, waiting for transfers between devices: 72.5 us -> none  [on_device(): lax.all_gather(hidden_share, 'seq', axis=1, tiled=True)]
    pmax x1 -> x0, blocking collectives: 57.1 us -> none  [on_device(): top_max = lax.pmax(run_max, 'seq')]
    cond x48 -> x0, local copies, waits for them, and re-layouts: 32.3 us -> none
  transfers between devices with their start and end apart: 7 -> 0, of which waited for: 7 -> 0; matrix products, arithmetic and copies ran while one was open for 2% -> 0% of each run, Pallas kernels for 0% -> 0%
where the time goes in v1:
time: 145 us
  Pallas kernels  144 us (99%)
  local copies, waits for them, and re-layouts  1.47 us (1%)
    pallas_call x1, Pallas kernels, finish_layer(): pl.pallas_call(finish_kernel, out_shape=jax.ShapeDtypeStruct((rows, local...  87.9 us
    pallas_call x1, Pallas kernels, project(): pl.pallas_call(project_kernel, out_shape=(jax.ShapeDtypeStruct((2, 2, NZ,...  38.4 us
    pallas_call x1, Pallas kernels, attend_pages(): pl.pallas_call(pages_kernel, grid_spec=pltpu.PrefetchScalarGridSpec(num_s...  17.3 us

profile of v1, /device:TPU:31, one launch (start us, length us, event | category | flops | bytes accessed | tf_op | source)
XLA Modules:
  0.0 145.1 jit_solution(5962707726875552251)
XLA Ops:
  0.0 38.4 %project.1 = (bf16[2,2,4,128,128]{4,3,2,1,0:T(8,128)(2,1)}, bf16[128,384]{1,0:T(8,128)(2,1)}) custom-call(bf16[128,256]{1,0:T(8,128)(2,1)} %bitcast.7, f32[1,256]{1,0:T(1,128)} %bitcast.12, bf16[3,256,2048]{2,1,0:T(8,128)(2,1)} %bitcast.6), custom_call_target="tpu_custom_call" | custom-call | tf_op jit(solution)/shard_map/project/pallas_call | solution.py:434
  38.4 17.3 %attend_pages.1 = (bf16[16,64,128]{2,1,0:T(8,128)(2,1)}, f32[16,8,128]{2,1,0:T(8,128)}) custom-call(s32[32]{0:T(128)} %owners.1, s32[32]{0:T(128)} %numbers.1, s32[64]{0:T(128)} %lengths.1, bf16[2,2,4,128,128]{4,3,2,1,0:T(8,128)(2,1)} %get-tuple-element.10.q_all, f32[1,16]{1,0:T(1,128)} %bitcast.10, bf16[32,64,2048]{2,1,0:T(8,128)(2,1)} %keys.1, ...), custom_call_target="tpu_custom_call" | custom-call | tf_op jit(solution)/shard_map/attend_pages/pallas_call | solution.py:549
  55.7 87.9 %finish_layer.1 = bf16[128,256]{1,0:T(8,128)(2,1)} custom-call(bf16[128,256]{1,0:T(8,128)(2,1)} %bitcast.8, bf16[128,384]{1,0:T(8,128)(2,1)} %get-tuple-element.9.qkv, f32[1,16]{1,0:T(1,128)} %bitcast.11, f32[1,256]{1,0:T(1,128)} %bitcast.13, bf16[16,64,128]{2,1,0:T(8,128)(2,1)} %get-tuple-element.11.page_out, f32[16,8,128]{2,1,0:T(8,128)} %get-tuple-element.12.marks, ...), custom_call_target="tpu_custom_call" | custom-call | tf_op jit(solution)/shard_map/finish_layer/pallas_call | solution.py:757
  143.6 1.5 %copy.15 = bf16[2,64,256]{2,1,0:T(8,128)(2,1)} copy(bf16[2,64,256]{2,1,0:T(8,128)(2,1)} %bitcast.9) | data formatting | bytes 131072

commit v2 on v1

--- a/solution.py
+++ b/solution.py
@@ -192,7 +192,7 @@
 MESH = pl.DeviceIdType.MESH
 NSEQ = 16
 NZ = 4
-CHUNKS = 2
+COPIES = 3 * NZ - 1
 VMEM_LIMIT = 60 * 1024 * 1024
 
 
@@ -268,114 +268,114 @@
     return row_to_column(mean), row_to_column(lax.rsqrt(variance + eps_norm))
 
 
-def row_chunks(rows):
-    size = rows // CHUNKS
-    return [pl.ds(k * size, size) for k in range(CHUNKS)]
-
-
 def add_into(target, extra):
     target[...] = (target[...].astype(jnp.float32) + extra[...].astype(jnp.float32)).astype(
         jnp.bfloat16
     )
 
 
-def reduce_scatter(parts, from_core, from_y, from_z, send_sem, recv_sem, finish):
+def reduce_scatter(parts, from_core, from_y, from_z, send_sem, recv_sem, produce):
     me, z, y, c = place()
-    chunks = row_chunks(parts.shape[3])
-    copies = []
-    first = []
-    for k, rows in enumerate(chunks):
-        sem = 5 * k
+    turns = [(z + 1 + turn) % NZ for turn in range(NZ)]
+    first, second, third = [], [], []
+    for turn, to in enumerate(turns):
+        produce(1 - c, to)
         first.append(
             send(
-                parts.at[1 - c, :, :, rows],
-                from_core.at[:, :, rows],
-                send_sem.at[sem],
-                recv_sem.at[sem],
+                parts.at[1 - c, to],
+                from_core.at[to],
+                send_sem.at[turn],
+                recv_sem.at[turn],
                 me + 1 - 2 * c,
             )
         )
-    second = []
-    for k, rows in enumerate(chunks):
-        first[k].wait_recv()
-        for zz in range(NZ):
-            add_into(parts.at[c, 1 - y, zz, rows], from_core.at[1 - y, zz, rows])
-        sem = 5 * k + 1
+    for to in turns:
+        produce(c, to)
+
+    def pass_z(turn):
+        to = turns[turn]
+        second[turn].wait_recv()
+        add_into(parts.at[c, to, y], from_y.at[to])
+        third.append(
+            send(
+                parts.at[c, to, y],
+                from_z.at[turn],
+                send_sem.at[2 * NZ + turn],
+                recv_sem.at[2 * NZ + turn],
+                to * 4 + y * 2 + c,
+            )
+        )
+
+    for turn, to in enumerate(turns):
+        first[turn].wait_recv()
+        add_into(parts.at[c, to, 1 - y], from_core.at[to, 1 - y])
         second.append(
             send(
-                parts.at[c, 1 - y, :, rows],
-                from_y.at[:, rows],
-                send_sem.at[sem],
-                recv_sem.at[sem],
+                parts.at[c, to, 1 - y],
+                from_y.at[to],
+                send_sem.at[NZ + turn],
+                recv_sem.at[NZ + turn],
                 me + 2 - 4 * y,
             )
         )
-        for zz in range(NZ):
-            add_into(parts.at[c, y, zz, rows], from_core.at[y, zz, rows])
-    third = []
-    for k, rows in enumerate(chunks):
-        second[k].wait_recv()
-        sent = []
-        for step in range(1, NZ):
-            to = (z + step) % NZ
-            add_into(parts.at[c, y, to, rows], from_y.at[to, rows])
-            sem = 5 * k + 1 + step
-            sent.append(
-                send(
-                    parts.at[c, y, to, rows],
-                    from_z.at[step - 1, rows],
-                    send_sem.at[sem],
-                    recv_sem.at[sem],
-                    to * 4 + y * 2 + c,
-                )
-            )
-        third.append(sent)
-    for k, rows in enumerate(chunks):
-        total = parts[c, y, z, rows].astype(jnp.float32) + from_y[z, rows].astype(jnp.float32)
-        for step in range(1, NZ):
-            third[k][step - 1].wait_recv()
-            total = total + from_z[step - 1, rows].astype(jnp.float32)
-        finish(k, rows, total)
-        copies += third[k]
-    return first + second + copies
-
-
-def all_gather(blocks, send_sem, recv_sem):
+        if turn < NZ - 1:
+            add_into(parts.at[c, to, y], from_core.at[to, y])
+        if turn > 0:
+            pass_z(turn - 1)
+    second[NZ - 1].wait_recv()
+    total = (
+        parts[c, z, y].astype(jnp.float32)
+        + from_core[z, y].astype(jnp.float32)
+        + from_y[z].astype(jnp.float32)
+    )
+    for turn in range(NZ - 1):
+        third[turn].wait_recv()
+        total = total + from_z[turn].astype(jnp.float32)
+    return total, first + second + third
+
+
+def all_gather(blocks, send_sem, recv_sem, consume):
     me, z, y, c = place()
-    chunks = row_chunks(blocks.shape[3])
-    first = []
-    for k, rows in enumerate(chunks):
-        own = blocks.at[c, y, z, rows]
-        first.append(
-            [
-                send(
-                    own,
-                    own,
-                    send_sem.at[5 * k + step - 1],
-                    recv_sem.at[5 * k + step - 1],
-                    ((z + step) % NZ) * 4 + y * 2 + c,
-                )
-                for step in range(1, NZ)
-            ]
-        )
-    second = []
-    for k, rows in enumerate(chunks):
-        for copy in first[k]:
-            copy.wait_recv()
-        own = blocks.at[c, y, :, rows]
-        second.append(
-            send(own, own, send_sem.at[5 * k + 3], recv_sem.at[5 * k + 3], me + 2 - 4 * y)
-        )
-    third = []
-    for k, rows in enumerate(chunks):
-        second[k].wait_recv()
-        own = blocks.at[c, :, :, rows]
-        third.append(
-            send(own, own, send_sem.at[5 * k + 4], recv_sem.at[5 * k + 4], me + 1 - 2 * c)
-        )
-    for copy in third:
-        copy.wait_recv()
-    return [copy for group in first for copy in group] + second + third
+    own = blocks.at[c, z, y]
+    turns = [(z + NZ - turn) % NZ for turn in range(NZ)]
+    along_z = [
+        send(
+            own,
+            own,
+            send_sem.at[turn - 1],
+            recv_sem.at[turn - 1],
+            ((z + turn) % NZ) * 4 + y * 2 + c,
+        )
+        for turn in range(1, NZ)
+    ]
+    along_y, across = [], []
+
+    def pass_y(turn):
+        block = blocks.at[c, turns[turn], y]
+        sem = NZ - 1 + turn
+        along_y.append(send(block, block, send_sem.at[sem], recv_sem.at[sem], me + 2 - 4 * y))
+
+    def pass_core(turn):
+        along_y[turn].wait_recv()
+        block = blocks.at[c, turns[turn]]
+        sem = 2 * NZ - 1 + turn
+        across.append(send(block, block, send_sem.at[sem], recv_sem.at[sem], me + 1 - 2 * c))
+        consume(c, turns[turn])
+
+    pass_y(0)
+    for turn in range(1, NZ):
+        along_z[turn - 1].wait_recv()
+        pass_y(turn)
+        pass_core(turn - 1)
+    pass_core(NZ - 1)
+    for turn in range(NZ):
+        across[turn].wait_recv()
+        consume(1 - c, turns[turn])
+    return along_z + along_y + across
+
+
+def columns_of(core, to, y, width):
+    return pl.ds(pl.multiple_of((to * 4 + y * 2 + core) * width, width), width)
 
 
 def project_kernel(
@@ -407,20 +407,25 @@
     mean, scale = finish_stats(stat_copies, stats)
     normed = ((token_float - mean) * scale * gain[...]).astype(jnp.bfloat16)
     load.wait()
-    for head in range(NSEQ):
-        columns = pl.ds(head * 128, 128)
-        for part in range(3):
-            parts[head % 2, (head // 2) % 2, head // 4, :, part * 128 : part * 128 + 128] = jnp.dot(
-                normed, w_qkv[part, :, columns], preferred_element_type=jnp.float32
+
+    def produce(core, to):
+        for side in range(2):
+            columns = columns_of(core, to, side, 128)
+            weight = jnp.concatenate([w_qkv[part, :, columns] for part in range(3)], axis=1)
+            parts[core, to, side] = jnp.dot(
+                normed, weight, preferred_element_type=jnp.float32
             ).astype(jnp.bfloat16)
 
-    def finish(k, rows, total):
-        joined = total.astype(jnp.bfloat16)
-        q_all[c, y, z, rows] = joined[:, :128]
-        kv_own[rows] = joined
-
-    copies = reduce_scatter(parts, from_core, from_y, from_z, rs_send, rs_recv, finish)
-    copies += all_gather(q_all, ag_send, ag_recv)
+    def consume(core, source):
+        del core, source
+
+    total, copies = reduce_scatter(
+        parts, from_core, from_y, from_z, rs_send, rs_recv, produce
+    )
+    joined = total.astype(jnp.bfloat16)
+    q_all[c, z, y] = joined[:, :128]
+    copies += all_gather(q_all, ag_send, ag_recv, consume)
+    kv_own[...] = joined
     for copy in stat_copies + copies:
         copy.wait_send()
 
@@ -434,7 +439,7 @@
     return pl.pallas_call(
         project_kernel,
         out_shape=(
-            jax.ShapeDtypeStruct((2, 2, NZ, rows, 128), bf16),
+            jax.ShapeDtypeStruct((2, NZ, 2, rows, 128), bf16),
             jax.ShapeDtypeStruct((rows, width), bf16),
         ),
         in_specs=[vmem, vmem, pl.BlockSpec(memory_space=pl.ANY)],
@@ -442,16 +447,16 @@
         scratch_shapes=[
             pltpu.VMEM(w_qkv.shape, bf16),
             pltpu.VMEM((NSEQ, 16, rows), jnp.float32),
-            pltpu.VMEM((2, 2, NZ, rows, width), bf16),
-            pltpu.VMEM((2, NZ, rows, width), bf16),
+            pltpu.VMEM((2, NZ, 2, rows, width), bf16),
+            pltpu.VMEM((NZ, 2, rows, width), bf16),
             pltpu.VMEM((NZ, rows, width), bf16),
             pltpu.VMEM((NZ - 1, rows, width), bf16),
             dma((NSEQ - 1,)),
             dma((NSEQ - 1,)),
-            dma((5 * CHUNKS,)),
-            dma((5 * CHUNKS,)),
-            dma((5 * CHUNKS,)),
-            dma((5 * CHUNKS,)),
+            dma((COPIES,)),
+            dma((COPIES,)),
+            dma((COPIES,)),
+            dma((COPIES,)),
             dma,
         ],
         compiler_params=pltpu.CompilerParams(
@@ -464,82 +469,112 @@
 PAGES_STEP = 8
 
 
-def pages_kernel(owners, numbers, lengths, q_all, slopes, keys, values, out, marks, q_rows):
+def pages_kernel(
+    owners, numbers, lengths, q_all, slopes, keys, values, out, marks, q_rows, tops, totals, owned
+):
     turn = pl.program_id(0)
     requests = lengths.shape[0]
     nheads = NSEQ
-    width = nheads * 128
     page_len = keys.shape[1]
     root = 128 ** (-0.5)
+    group = 4
+    ngroups = nheads // group
+    width = group * 128
+    count = 2 * nheads
 
     @pl.when(turn == 0)
     def _():
         for head in range(nheads):
             q_rows[:, head * 128 : head * 128 + 128] = q_all[
-                head % 2, (head // 2) % 2, head // 4
+                head % 2, head // 4, (head // 2) % 2
             ].astype(jnp.float32)
-        marks[...] = jnp.full_like(marks, -1.0)
-
-    own_head = lax.broadcasted_iota(jnp.int32, (nheads, width), 0) == (
-        lax.broadcasted_iota(jnp.int32, (nheads, width), 1) // 128
-    )
+        tops[...] = jnp.zeros_like(tops)
+        totals[...] = jnp.zeros_like(totals)
+        owned[...] = jnp.full_like(owned, -1.0)
+
+    spot = lax.broadcasted_iota(jnp.int32, (2 * group, width), 0)
+    own_head = spot % group == lax.broadcasted_iota(jnp.int32, (2 * group, width), 1) // 128
+    first_step = spot < group
+    row = lax.broadcasted_iota(jnp.int32, (count, nheads), 0)
+    row_head = row // (2 * group) * group + row % group
     slope = jnp.sum(
         jnp.where(
-            lax.broadcasted_iota(jnp.int32, (nheads, nheads), 0)
-            == lax.broadcasted_iota(jnp.int32, (nheads, nheads), 1),
-            slopes[...],
-            0.0,
+            row_head == lax.broadcasted_iota(jnp.int32, (count, nheads), 1), slopes[...], 0.0
         ),
         axis=1,
         keepdims=True,
     )
-    slope = jnp.concatenate([slope, slope], axis=0)
-    step_row = lax.broadcasted_iota(jnp.int32, (2 * nheads, page_len), 0) // nheads
-    offset = lax.broadcasted_iota(jnp.int32, (2 * nheads, page_len), 1)
-    lane = lax.broadcasted_iota(jnp.int32, (nheads, 128), 1)
-    top_rows = marks[:, 0, :]
-    sum_rows = marks[:, 1, :]
-    owner_rows = marks[:, 2, :]
+    step_row = lax.broadcasted_iota(jnp.int32, (count, page_len), 0) // group % 2
+    offset = lax.broadcasted_iota(jnp.int32, (count, page_len), 1)
+    lane = lax.broadcasted_iota(jnp.int32, (count, 128), 1)
+    lane_step = lax.broadcasted_iota(jnp.int32, (count, 128), 0) // group % 2
+    lane_one = lax.broadcasted_iota(jnp.int32, (1, 128), 1)
+    top_rows = tops[...]
+    sum_rows = totals[...]
+    owner_row = owned[0:1, :]
     page_outs = []
     for slot in range(PAGES_STEP):
         page = turn * PAGES_STEP + slot
         owner = owners[page]
         safe = jnp.clip(owner, 0, requests - 1)
         left = lengths[safe] - numbers[page] * page_len
-        queries = [
-            jnp.where(own_head, q_rows[pl.ds(safe + step * requests, 1), :], 0.0)
-            for step in range(2)
-        ]
-        spread = jnp.concatenate(queries, axis=0).astype(jnp.bfloat16)
-        scores = lax.dot_general(
-            spread, keys[slot], (((1,), (1,)), ((), ())), preferred_element_type=jnp.float32
-        )
+        q_first = q_rows[pl.ds(safe, 1), :]
+        q_second = q_rows[pl.ds(safe + requests, 1), :]
+        scores = []
+        for g in range(ngroups):
+            columns = slice(g * width, (g + 1) * width)
+            spread = jnp.where(
+                own_head, jnp.where(first_step, q_first[:, columns], q_second[:, columns]), 0.0
+            ).astype(jnp.bfloat16)
+            scores.append(
+                lax.dot_general(
+                    spread,
+                    keys[slot, :, columns],
+                    (((1,), (1,)), ((), ())),
+                    preferred_element_type=jnp.float32,
+                )
+            )
         distance = (left + step_row - offset).astype(jnp.float32)
-        scores = scores * root - distance * slope
+        score = jnp.concatenate(scores, axis=0) * root - distance * slope
         valid = (offset < left) & (owner >= 0)
-        masked = jnp.where(valid, scores, floor_score)
+        masked = jnp.where(valid, score, floor_score)
         top = jnp.max(masked, axis=1, keepdims=True)
         expon = jnp.where(valid, jnp.exp(masked - top), 0.0)
         total = jnp.sum(expon, axis=1, keepdims=True)
-        mixed = jnp.dot(
-            expon.astype(jnp.bfloat16), values[slot], preferred_element_type=jnp.float32
-        )
-        for step in range(2):
-            rows = slice(step * nheads, (step + 1) * nheads)
-            page_outs.append(
-                jnp.sum(jnp.where(own_head, mixed[rows], 0.0), axis=0, keepdims=True)
+        mixed = []
+        for g in range(ngroups):
+            product = jnp.dot(
+                expon[g * 2 * group : (g + 1) * 2 * group].astype(jnp.bfloat16),
+                values[slot, :, g * width : (g + 1) * width],
+                preferred_element_type=jnp.float32,
             )
-            here = lane == 2 * page + step
-            top_rows = jnp.where(here, top[rows], top_rows)
-            sum_rows = jnp.where(here, total[rows], sum_rows)
-            owner_rows = jnp.where(here, owner.astype(jnp.float32), owner_rows)
-    marks[:, 0, :] = top_rows
-    marks[:, 1, :] = sum_rows
-    marks[:, 2, :] = owner_rows
+            mixed.append(jnp.where(own_head, product, 0.0))
+        mixed = jnp.concatenate(mixed, axis=1)
+        page_outs.append(jnp.sum(mixed[:group], axis=0, keepdims=True))
+        page_outs.append(jnp.sum(mixed[group:], axis=0, keepdims=True))
+        here = lane == 2 * page + lane_step
+        top_rows = jnp.where(here, top, top_rows)
+        sum_rows = jnp.where(here, total, sum_rows)
+        owner_row = jnp.where(lane_one // 2 == page, owner.astype(jnp.float32), owner_row)
+    tops[...] = top_rows
+    totals[...] = sum_rows
+    owned[0:1, :] = owner_row
     stacked = jnp.concatenate(page_outs, axis=0).astype(jnp.bfloat16)
     first = pl.multiple_of(turn * 2 * PAGES_STEP, 2 * PAGES_STEP)
     for head in range(nheads):
         out[head, pl.ds(first, 2 * PAGES_STEP), :] = stacked[:, head * 128 : head * 128 + 128]
+
+    @pl.when(turn == pl.num_programs(0) - 1)
+    def _():
+        even = lane_one % 2 == 0
+        for head in range(nheads):
+            at = head // group * 2 * group + head % group
+            for n, rows in enumerate((top_rows, sum_rows)):
+                marks[head, n : n + 1, :] = jnp.where(
+                    even, rows[at : at + 1], rows[at + group : at + group + 1]
+                )
+            marks[head, 2:3, :] = owner_row
+            marks[head, 3:8, :] = jnp.zeros((5, 128), jnp.float32)
 
 
 def attend_pages(page_owner, page_number, lengths, q_all, slopes, key_pages, value_pages):
@@ -561,7 +596,12 @@
                 pl.BlockSpec((NSEQ, 2 * npages, 128), lambda i, *_: (0, 0, 0)),
                 pl.BlockSpec((NSEQ, 8, 128), lambda i, *_: (0, 0, 0)),
             ),
-            scratch_shapes=[pltpu.VMEM((rows, width), jnp.float32)],
+            scratch_shapes=[
+                pltpu.VMEM((rows, width), jnp.float32),
+                pltpu.VMEM((2 * NSEQ, 128), jnp.float32),
+                pltpu.VMEM((2 * NSEQ, 128), jnp.float32),
+                pltpu.VMEM((8, 128), jnp.float32),
+            ],
         ),
         out_shape=(
             jax.ShapeDtypeStruct((NSEQ, 2 * npages, 128), jnp.bfloat16),
@@ -685,18 +725,22 @@
     got_marks[me] = marks[me]
     for copy in copies:
         copy.wait_recv()
-    attended[c, y, z] = combine(qkv, slopes, got_out, got_marks)
-    copies += all_gather(attended, ag_send.at[0], ag_recv.at[0])
+    attended[c, z, y] = combine(qkv, slopes, got_out, got_marks)
     contract = (((1,), (1,)), ((), ()))
+    sums = [jnp.zeros(result.shape, jnp.float32), jnp.zeros(result.shape, jnp.float32)]
     loads[0].wait()
-    projected = jnp.zeros(pair_out.shape[2:], jnp.float32)
-    for head in range(NSEQ):
-        projected = projected + lax.dot_general(
-            attended[head % 2, (head // 2) % 2, head // 4],
-            w_out[:, head * 128 : head * 128 + 128],
-            contract,
-            preferred_element_type=jnp.float32,
-        )
+
+    def consume_attended(core, source):
+        for side in range(2):
+            sums[0] = sums[0] + lax.dot_general(
+                attended[core, source, side],
+                w_out[:, columns_of(core, source, side, 128)],
+                contract,
+                preferred_element_type=jnp.float32,
+            )
+
+    copies += all_gather(attended, ag_send.at[0], ag_recv.at[0], consume_attended)
+    projected = sums[0].astype(jnp.bfloat16)
     pair_out[0, 0] = projected
     pair = send(
         pair_out.at[0, 0], pair_out.at[0, 1], pair_send.at[0], pair_recv.at[0], other, "head"
@@ -704,7 +748,7 @@
     copies.append(pair)
     pair.wait_recv()
     hidden_in = (
-        tokens[...].astype(jnp.float32) + (projected + pair_out[0, 1])
+        tokens[...].astype(jnp.float32) + (projected.astype(jnp.float32) + pair_out[0, 1].astype(jnp.float32))
     ).astype(jnp.bfloat16)
     hidden_float = hidden_in.astype(jnp.float32)
     stat_copies = start_stats(hidden_float, stats, stat_send, stat_recv)
@@ -713,36 +757,37 @@
     normed = ((hidden_float - mean) * scale * gain[...]).astype(jnp.bfloat16)
     loads[1].wait()
     share = parts.shape[4]
-    for block in range(NSEQ):
-        parts[block % 2, (block // 2) % 2, block // 4] = jnp.dot(
-            normed,
-            w_up[:, block * share : (block + 1) * share],
-            preferred_element_type=jnp.float32,
-        ).astype(jnp.bfloat16)
-
-    def finish(k, rows, total):
-        hidden[c, y, z, rows] = (0.5 * total * (1.0 + lax.erf(total * 0.5**0.5))).astype(
-            jnp.bfloat16
-        )
-
-    copies += reduce_scatter(parts, from_core, from_y, from_z, rs_send, rs_recv, finish)
-    copies += all_gather(hidden, ag_send.at[1], ag_recv.at[1])
+
+    def produce(core, to):
+        for side in range(2):
+            parts[core, to, side] = jnp.dot(
+                normed,
+                w_up[:, columns_of(core, to, side, share)],
+                preferred_element_type=jnp.float32,
+            ).astype(jnp.bfloat16)
+
+    def consume_hidden(core, source):
+        for side in range(2):
+            sums[1] = sums[1] + lax.dot_general(
+                hidden[core, source, side],
+                w_down[:, columns_of(core, source, side, share)],
+                contract,
+                preferred_element_type=jnp.float32,
+            )
+
+    total, sent = reduce_scatter(parts, from_core, from_y, from_z, rs_send, rs_recv, produce)
+    copies += sent
+    hidden[c, z, y] = (0.5 * total * (1.0 + lax.erf(total * 0.5**0.5))).astype(jnp.bfloat16)
     loads[2].wait()
-    down = jnp.zeros(pair_out.shape[2:], jnp.float32)
-    for block in range(NSEQ):
-        down = down + lax.dot_general(
-            hidden[block % 2, (block // 2) % 2, block // 4],
-            w_down[:, block * share : (block + 1) * share],
-            contract,
-            preferred_element_type=jnp.float32,
-        )
+    copies += all_gather(hidden, ag_send.at[1], ag_recv.at[1], consume_hidden)
+    down = sums[1].astype(jnp.bfloat16)
     pair_out[1, 0] = down
     pair = send(
         pair_out.at[1, 0], pair_out.at[1, 1], pair_send.at[1], pair_recv.at[1], other, "head"
     )
     copies.append(pair)
     pair.wait_recv()
-    result[...] = (hidden_float + (down + pair_out[1, 1])).astype(jnp.bfloat16)
+    result[...] = (hidden_float + (down.astype(jnp.float32) + pair_out[1, 1].astype(jnp.float32))).astype(jnp.bfloat16)
     for copy in copies:
         copy.wait_send()
 
@@ -765,24 +810,24 @@
             pltpu.VMEM(w_down.shape, bf16),
             pltpu.VMEM(page_out.shape, bf16),
             pltpu.VMEM(marks.shape, jnp.float32),
-            pltpu.VMEM((2, 2, NZ, rows, 128), bf16),
-            pltpu.VMEM((2, 2, rows, local_width), jnp.float32),
+            pltpu.VMEM((2, NZ, 2, rows, 128), bf16),
+            pltpu.VMEM((2, 2, rows, local_width), bf16),
             pltpu.VMEM((NSEQ, 16, rows), jnp.float32),
-            pltpu.VMEM((2, 2, NZ, rows, share), bf16),
-            pltpu.VMEM((2, NZ, rows, share), bf16),
+            pltpu.VMEM((2, NZ, 2, rows, share), bf16),
+            pltpu.VMEM((NZ, 2, rows, share), bf16),
             pltpu.VMEM((NZ, rows, share), bf16),
             pltpu.VMEM((NZ - 1, rows, share), bf16),
-            pltpu.VMEM((2, 2, NZ, rows, share), bf16),
+            pltpu.VMEM((2, NZ, 2, rows, share), bf16),
             dma((2 * NSEQ - 2,)),
             dma((2 * NSEQ - 2,)),
             dma((2,)),
             dma((2,)),
             dma((NSEQ - 1,)),
             dma((NSEQ - 1,)),
-            dma((5 * CHUNKS,)),
-            dma((5 * CHUNKS,)),
-            dma((2, 5 * CHUNKS)),
-            dma((2, 5 * CHUNKS)),
+            dma((COPIES,)),
+            dma((COPIES,)),
+            dma((2, COPIES)),
+            dma((2, COPIES)),
             dma((3,)),
         ],
         compiler_params=pltpu.CompilerParams(

time: 145 us -> 134 us (0.924)
  Pallas kernels: 144 us -> 132 us
    pallas_call x1, Pallas kernels: 87.9 us -> 82.1 us  [finish_layer(): pl.pallas_call(finish_kernel, out_shape=jax.ShapeDtypeStruct((rows, local...]
    pallas_call x1, Pallas kernels: 17.3 us -> 13.6 us  [attend_pages(): pl.pallas_call(pages_kernel, grid_spec=pltpu.PrefetchScalarGridSpec(num_s...]
    pallas_call x1, Pallas kernels: 38.4 us -> 35.8 us  [project(): pl.pallas_call(project_kernel, out_shape=(jax.ShapeDtypeStruct((2, NZ, 2,...]
where the time goes in v2:
time: 134 us; the launch traced here: 133 us
  Pallas kernels  132 us (99%)
  local copies, waits for them, and re-layouts  1.47 us (1%)
    pallas_call x1, Pallas kernels, finish_layer(): pl.pallas_call(finish_kernel, out_shape=jax.ShapeDtypeStruct((rows, local...  82.1 us
    pallas_call x1, Pallas kernels, project(): pl.pallas_call(project_kernel, out_shape=(jax.ShapeDtypeStruct((2, NZ, 2,...  35.8 us
    pallas_call x1, Pallas kernels, attend_pages(): pl.pallas_call(pages_kernel, grid_spec=pltpu.PrefetchScalarGridSpec(num_s...  13.6 us

profile of v2, /device:TPU:31, one launch (start us, length us, event | category | flops | bytes accessed | tf_op | source)
XLA Modules:
  0.0 133.0 jit_solution(3821365090580562391)
XLA Ops:
  0.0 35.8 %project.1 = (bf16[2,4,2,128,128]{4,3,2,1,0:T(8,128)(2,1)}, bf16[128,384]{1,0:T(8,128)(2,1)}) custom-call(bf16[128,256]{1,0:T(8,128)(2,1)} %bitcast.7, f32[1,256]{1,0:T(1,128)} %bitcast.12, bf16[3,256,2048]{2,1,0:T(8,128)(2,1)} %bitcast.6), custom_call_target="tpu_custom_call" | custom-call | tf_op jit(solution)/shard_map/project/pallas_call | solution.py:439
  35.8 13.6 %attend_pages.1 = (bf16[16,64,128]{2,1,0:T(8,128)(2,1)}, f32[16,8,128]{2,1,0:T(8,128)}) custom-call(s32[32]{0:T(128)} %owners.1, s32[32]{0:T(128)} %numbers.1, s32[64]{0:T(128)} %lengths.1, bf16[2,4,2,128,128]{4,3,2,1,0:T(8,128)(2,1)} %get-tuple-element.10.q_all, f32[1,16]{1,0:T(1,128)} %bitcast.10, bf16[32,64,2048]{2,1,0:T(8,128)(2,1)} %keys.1, ...), custom_call_target="tpu_custom_call" | custom-call | tf_op jit(solution)/shard_map/attend_pages/pallas_call | solution.py:584
  49.4 82.1 %finish_layer.1 = bf16[128,256]{1,0:T(8,128)(2,1)} custom-call(bf16[128,256]{1,0:T(8,128)(2,1)} %bitcast.8, bf16[128,384]{1,0:T(8,128)(2,1)} %get-tuple-element.9.qkv, f32[1,16]{1,0:T(1,128)} %bitcast.11, f32[1,256]{1,0:T(1,128)} %bitcast.13, bf16[16,64,128]{2,1,0:T(8,128)(2,1)} %get-tuple-element.11.page_out, f32[16,8,128]{2,1,0:T(8,128)} %get-tuple-element.12.marks, ...), custom_call_target="tpu_custom_call" | custom-call | tf_op jit(solution)/shard_map/finish_layer/pallas_call | solution.py:802
  131.5 1.5 %copy.15 = bf16[2,64,256]{2,1,0:T(8,128)(2,1)} copy(bf16[2,64,256]{2,1,0:T(8,128)(2,1)} %bitcast.9) | data formatting | bytes 131072

commit v3 on v2

--- a/solution.py
+++ b/solution.py
@@ -239,12 +239,10 @@
     me = lax.axis_index("seq")
     ones = jnp.ones((8, values.shape[1]), jnp.float32)
     contract = (((1,), (1,)), ((), ()))
-    stats[me, 0:8, :] = lax.dot_general(
-        ones, values, contract, precision=highest, preferred_element_type=jnp.float32
-    )
-    stats[me, 8:16, :] = lax.dot_general(
-        ones, values * values, contract, precision=highest, preferred_element_type=jnp.float32
-    )
+    for n, terms in enumerate((values, values * values)):
+        stats[me, n : n + 1, :] = lax.dot_general(
+            ones, terms, contract, precision=highest, preferred_element_type=jnp.float32
+        )[0:1]
     return [
         send(
             stats.at[me],
@@ -264,7 +262,7 @@
     for source in range(1, NSEQ):
         total = total + stats[source]
     mean = total[0:1, :] / D
-    variance = total[8:9, :] / D - mean * mean
+    variance = total[1:2, :] / D - mean * mean
     return row_to_column(mean), row_to_column(lax.rsqrt(variance + eps_norm))
 
 
@@ -274,64 +272,83 @@
     )
 
 
-def reduce_scatter(parts, from_core, from_y, from_z, send_sem, recv_sem, produce):
-    me, z, y, c = place()
-    turns = [(z + 1 + turn) % NZ for turn in range(NZ)]
-    first, second, third = [], [], []
-    for turn, to in enumerate(turns):
-        produce(1 - c, to)
-        first.append(
-            send(
-                parts.at[1 - c, to],
-                from_core.at[to],
-                send_sem.at[turn],
-                recv_sem.at[turn],
-                me + 1 - 2 * c,
-            )
-        )
-    for to in turns:
-        produce(c, to)
-
-    def pass_z(turn):
-        to = turns[turn]
-        second[turn].wait_recv()
-        add_into(parts.at[c, to, y], from_y.at[to])
-        third.append(
-            send(
-                parts.at[c, to, y],
-                from_z.at[turn],
-                send_sem.at[2 * NZ + turn],
-                recv_sem.at[2 * NZ + turn],
-                to * 4 + y * 2 + c,
-            )
-        )
-
-    for turn, to in enumerate(turns):
-        first[turn].wait_recv()
+class ReduceScatter:
+    def __init__(self, parts, from_core, from_y, from_z, send_sem, recv_sem, produce):
+        self.refs = parts, from_core, from_y, from_z
+        self.sems = send_sem, recv_sem
+        self.produce = produce
+        me, z, y, c = place()
+        self.turns = [(z + 1 + turn) % NZ for turn in range(NZ)]
+        self.first, self.second, self.third = [], [], []
+
+    def put(self, src, dst, sem, peer):
+        send_sem, recv_sem = self.sems
+        return send(src, dst, send_sem.at[sem], recv_sem.at[sem], peer)
+
+    def pass_core(self, turn):
+        me, z, y, c = place()
+        parts, from_core, from_y, from_z = self.refs
+        to = self.turns[turn]
+        self.produce(1 - c, to)
+        self.first.append(
+            self.put(parts.at[1 - c, to], from_core.at[to], turn, me + 1 - 2 * c)
+        )
+
+    def own(self):
+        me, z, y, c = place()
+        for to in self.turns:
+            self.produce(c, to)
+
+    def pass_y(self, turn):
+        me, z, y, c = place()
+        parts, from_core, from_y, from_z = self.refs
+        to = self.turns[turn]
+        self.first[turn].wait_recv()
         add_into(parts.at[c, to, 1 - y], from_core.at[to, 1 - y])
-        second.append(
-            send(
-                parts.at[c, to, 1 - y],
-                from_y.at[to],
-                send_sem.at[NZ + turn],
-                recv_sem.at[NZ + turn],
-                me + 2 - 4 * y,
-            )
+        self.second.append(
+            self.put(parts.at[c, to, 1 - y], from_y.at[to], NZ + turn, me + 2 - 4 * y)
         )
         if turn < NZ - 1:
             add_into(parts.at[c, to, y], from_core.at[to, y])
-        if turn > 0:
-            pass_z(turn - 1)
-    second[NZ - 1].wait_recv()
-    total = (
-        parts[c, z, y].astype(jnp.float32)
-        + from_core[z, y].astype(jnp.float32)
-        + from_y[z].astype(jnp.float32)
-    )
-    for turn in range(NZ - 1):
-        third[turn].wait_recv()
-        total = total + from_z[turn].astype(jnp.float32)
-    return total, first + second + third
+
+    def pass_z(self, turn):
+        me, z, y, c = place()
+        parts, from_core, from_y, from_z = self.refs
+        to = self.turns[turn]
+        self.second[turn].wait_recv()
+        add_into(parts.at[c, to, y], from_y.at[to])
+        self.third.append(
+            self.put(
+                parts.at[c, to, y], from_z.at[turn], 2 * NZ + turn, to * 4 + y * 2 + c
+            )
+        )
+
+    def collect(self):
+        me, z, y, c = place()
+        parts, from_core, from_y, from_z = self.refs
+        self.second[NZ - 1].wait_recv()
+        total = (
+            parts[c, z, y].astype(jnp.float32)
+            + from_core[z, y].astype(jnp.float32)
+            + from_y[z].astype(jnp.float32)
+        )
+        for turn in range(NZ - 1):
+            self.third[turn].wait_recv()
+            total = total + from_z[turn].astype(jnp.float32)
+        return total
+
+    def run(self):
+        for turn in range(NZ):
+            self.pass_core(turn)
+        self.own()
+        for turn in range(NZ):
+            self.pass_y(turn)
+            if turn > 0:
+                self.pass_z(turn - 1)
+        return self.collect()
+
+    def copies(self):
+        return self.first + self.second + self.third
 
 
 def all_gather(blocks, send_sem, recv_sem, consume):
@@ -378,101 +395,12 @@
     return pl.ds(pl.multiple_of((to * 4 + y * 2 + core) * width, width), width)
 
 
-def project_kernel(
-    tokens,
-    gain,
-    w_hbm,
-    q_all,
-    kv_own,
-    w_qkv,
-    stats,
-    parts,
-    from_core,
-    from_y,
-    from_z,
-    stat_send,
-    stat_recv,
-    rs_send,
-    rs_recv,
-    ag_send,
-    ag_recv,
-    load_sem,
+PAGES_STEP = 8
+
+
+def visit_pages(
+    turn, owners, numbers, lengths, slopes, keys, values, out, q_rows, tops, totals, owned
 ):
-    load = pltpu.make_async_copy(w_hbm, w_qkv, load_sem)
-    load.start()
-    me, z, y, c = place()
-    greet_all(False)
-    token_float = tokens[...].astype(jnp.float32)
-    stat_copies = start_stats(token_float, stats, stat_send, stat_recv)
-    mean, scale = finish_stats(stat_copies, stats)
-    normed = ((token_float - mean) * scale * gain[...]).astype(jnp.bfloat16)
-    load.wait()
-
-    def produce(core, to):
-        for side in range(2):
-            columns = columns_of(core, to, side, 128)
-            weight = jnp.concatenate([w_qkv[part, :, columns] for part in range(3)], axis=1)
-            parts[core, to, side] = jnp.dot(
-                normed, weight, preferred_element_type=jnp.float32
-            ).astype(jnp.bfloat16)
-
-    def consume(core, source):
-        del core, source
-
-    total, copies = reduce_scatter(
-        parts, from_core, from_y, from_z, rs_send, rs_recv, produce
-    )
-    joined = total.astype(jnp.bfloat16)
-    q_all[c, z, y] = joined[:, :128]
-    copies += all_gather(q_all, ag_send, ag_recv, consume)
-    kv_own[...] = joined
-    for copy in stat_copies + copies:
-        copy.wait_send()
-
-
-def project(tokens, gain, w_qkv):
-    rows = tokens.shape[0]
-    width = 384
-    vmem = pl.BlockSpec(memory_space=pltpu.VMEM)
-    dma = pltpu.SemaphoreType.DMA
-    bf16 = jnp.bfloat16
-    return pl.pallas_call(
-        project_kernel,
-        out_shape=(
-            jax.ShapeDtypeStruct((2, NZ, 2, rows, 128), bf16),
-            jax.ShapeDtypeStruct((rows, width), bf16),
-        ),
-        in_specs=[vmem, vmem, pl.BlockSpec(memory_space=pl.ANY)],
-        out_specs=(vmem, vmem),
-        scratch_shapes=[
-            pltpu.VMEM(w_qkv.shape, bf16),
-            pltpu.VMEM((NSEQ, 16, rows), jnp.float32),
-            pltpu.VMEM((2, NZ, 2, rows, width), bf16),
-            pltpu.VMEM((NZ, 2, rows, width), bf16),
-            pltpu.VMEM((NZ, rows, width), bf16),
-            pltpu.VMEM((NZ - 1, rows, width), bf16),
-            dma((NSEQ - 1,)),
-            dma((NSEQ - 1,)),
-            dma((COPIES,)),
-            dma((COPIES,)),
-            dma((COPIES,)),
-            dma((COPIES,)),
-            dma,
-        ],
-        compiler_params=pltpu.CompilerParams(
-            collective_id=0, has_side_effects=True, vmem_limit_bytes=VMEM_LIMIT
-        ),
-        name="project",
-    )(tokens, gain, w_qkv)
-
-
-PAGES_STEP = 8
-
-
-def pages_kernel(
-    owners, numbers, lengths, q_all, slopes, keys, values, out, marks, q_rows, tops, totals, owned
-):
-    turn = pl.program_id(0)
     requests = lengths.shape[0]
     nheads = NSEQ
     page_len = keys.shape[1]
@@ -481,16 +409,6 @@
     ngroups = nheads // group
     width = group * 128
     count = 2 * nheads
-
-    @pl.when(turn == 0)
-    def _():
-        for head in range(nheads):
-            q_rows[:, head * 128 : head * 128 + 128] = q_all[
-                head % 2, head // 4, (head // 2) % 2
-            ].astype(jnp.float32)
-        tops[...] = jnp.zeros_like(tops)
-        totals[...] = jnp.zeros_like(totals)
-        owned[...] = jnp.full_like(owned, -1.0)
 
     spot = lax.broadcasted_iota(jnp.int32, (2 * group, width), 0)
     own_head = spot % group == lax.broadcasted_iota(jnp.int32, (2 * group, width), 1) // 128
@@ -529,7 +447,7 @@
             scores.append(
                 lax.dot_general(
                     spread,
-                    keys[slot, :, columns],
+                    keys[page, :, columns],
                     (((1,), (1,)), ((), ())),
                     preferred_element_type=jnp.float32,
                 )
@@ -545,7 +463,7 @@
         for g in range(ngroups):
             product = jnp.dot(
                 expon[g * 2 * group : (g + 1) * 2 * group].astype(jnp.bfloat16),
-                values[slot, :, g * width : (g + 1) * width],
+                values[page, :, g * width : (g + 1) * width],
                 preferred_element_type=jnp.float32,
             )
             mixed.append(jnp.where(own_head, product, 0.0))
@@ -564,54 +482,18 @@
     for head in range(nheads):
         out[head, pl.ds(first, 2 * PAGES_STEP), :] = stacked[:, head * 128 : head * 128 + 128]
 
-    @pl.when(turn == pl.num_programs(0) - 1)
-    def _():
-        even = lane_one % 2 == 0
-        for head in range(nheads):
-            at = head // group * 2 * group + head % group
-            for n, rows in enumerate((top_rows, sum_rows)):
-                marks[head, n : n + 1, :] = jnp.where(
-                    even, rows[at : at + 1], rows[at + group : at + group + 1]
-                )
-            marks[head, 2:3, :] = owner_row
-            marks[head, 3:8, :] = jnp.zeros((5, 128), jnp.float32)
-
-
-def attend_pages(page_owner, page_number, lengths, q_all, slopes, key_pages, value_pages):
-    npages, page_len, width = key_pages.shape
-    rows = q_all.shape[3]
-    block = pl.BlockSpec((PAGES_STEP, page_len, width), lambda i, *_: (i, 0, 0))
-    return pl.pallas_call(
-        pages_kernel,
-        grid_spec=pltpu.PrefetchScalarGridSpec(
-            num_scalar_prefetch=3,
-            grid=(npages // PAGES_STEP,),
-            in_specs=[
-                pl.BlockSpec(q_all.shape, lambda i, *_: (0, 0, 0, 0, 0)),
-                pl.BlockSpec(slopes.shape, lambda i, *_: (0, 0)),
-                block,
-                block,
-            ],
-            out_specs=(
-                pl.BlockSpec((NSEQ, 2 * npages, 128), lambda i, *_: (0, 0, 0)),
-                pl.BlockSpec((NSEQ, 8, 128), lambda i, *_: (0, 0, 0)),
-            ),
-            scratch_shapes=[
-                pltpu.VMEM((rows, width), jnp.float32),
-                pltpu.VMEM((2 * NSEQ, 128), jnp.float32),
-                pltpu.VMEM((2 * NSEQ, 128), jnp.float32),
-                pltpu.VMEM((8, 128), jnp.float32),
-            ],
-        ),
-        out_shape=(
-            jax.ShapeDtypeStruct((NSEQ, 2 * npages, 128), jnp.bfloat16),
-            jax.ShapeDtypeStruct((NSEQ, 8, 128), jnp.float32),
-        ),
-        compiler_params=pltpu.CompilerParams(
-            vmem_limit_bytes=VMEM_LIMIT, dimension_semantics=("arbitrary",)
-        ),
-        name="attend_pages",
-    )(page_owner, page_number, lengths, q_all, slopes, key_pages, value_pages)
+
+def write_marks(marks, tops, totals, owned):
+    group = 4
+    even = lax.broadcasted_iota(jnp.int32, (1, 128), 1) % 2 == 0
+    for head in range(NSEQ):
+        at = head // group * 2 * group + head % group
+        for n, rows in enumerate((tops[...], totals[...])):
+            marks[head, n : n + 1, :] = jnp.where(
+                even, rows[at : at + 1], rows[at + group : at + group + 1]
+            )
+        marks[head, 2:3, :] = owned[0:1, :]
+        marks[head, 3:4, :] = jnp.zeros((1, 128), jnp.float32)
 
 
 def combine(qkv, slopes, page_out, marks):
@@ -664,24 +546,48 @@
     return (mixed / total).astype(jnp.bfloat16)
 
 
-def finish_kernel(
+def layer_kernel(
+    owners,
+    numbers,
+    lengths,
     tokens,
-    qkv,
     slopes,
+    gain_one,
     gain,
-    page_out,
-    marks,
+    w_qkv_hbm,
+    keys_hbm,
+    values_hbm,
     w_out_hbm,
     w_up_hbm,
     w_down_hbm,
     result,
+    w_qkv,
+    keys,
+    values,
     w_out,
     w_up,
     w_down,
+    q_parts,
+    q_core,
+    q_y,
+    q_z,
+    kv_parts,
+    kv_core,
+    kv_y,
+    kv_z,
+    q_all,
+    qkv,
+    q_rows,
+    tops,
+    totals,
+    owned,
+    page_out,
+    marks,
     got_out,
     got_marks,
     attended,
     pair_out,
+    stats_one,
     stats,
     parts,
     from_core,
@@ -699,7 +605,19 @@
     ag_send,
     ag_recv,
     load_sem,
+    page_sem,
 ):
+    load_qkv = pltpu.make_async_copy(w_qkv_hbm, w_qkv, load_sem.at[3])
+    load_qkv.start()
+    npages = keys.shape[0]
+    nturns = npages // PAGES_STEP
+    page_loads = []
+    for turn in range(nturns):
+        some = pl.ds(turn * PAGES_STEP, PAGES_STEP)
+        for n, (src, dst) in enumerate(((keys_hbm, keys), (values_hbm, values))):
+            load = pltpu.make_async_copy(src.at[some], dst.at[some], page_sem.at[turn, n])
+            load.start()
+            page_loads.append(load)
     loads = [
         pltpu.make_async_copy(src, dst, load_sem.at[n])
         for n, (src, dst) in enumerate(
@@ -711,19 +629,93 @@
     me, z, y, c = place()
     other = 1 - lax.axis_index("head")
     greet_all(True)
-    copies = []
-    for step in range(1, NSEQ):
-        to = (me + step) % NSEQ
-        n = 2 * (step - 1)
-        copies.append(
-            send(page_out.at[to], got_out.at[me], ex_send.at[n], ex_recv.at[n], to)
-        )
-        copies.append(
-            send(marks.at[to], got_marks.at[me], ex_send.at[n + 1], ex_recv.at[n + 1], to)
-        )
+    token_float = tokens[...].astype(jnp.float32)
+    copies = start_stats(token_float, stats_one, stat_send.at[0], stat_recv.at[0])
+    mean, scale = finish_stats(copies, stats_one)
+    normed_one = ((token_float - mean) * scale * gain_one[...]).astype(jnp.bfloat16)
+    load_qkv.wait()
+
+    def produce_q(core, to):
+        for side in range(2):
+            q_parts[core, to, side] = jnp.dot(
+                normed_one,
+                w_qkv[0, :, columns_of(core, to, side, 128)],
+                preferred_element_type=jnp.float32,
+            ).astype(jnp.bfloat16)
+
+    def produce_kv(core, to):
+        for side in range(2):
+            columns = columns_of(core, to, side, 128)
+            weight = jnp.concatenate([w_qkv[1, :, columns], w_qkv[2, :, columns]], axis=1)
+            kv_parts[core, to, side] = jnp.dot(
+                normed_one, weight, preferred_element_type=jnp.float32
+            ).astype(jnp.bfloat16)
+
+    q_sum = ReduceScatter(q_parts, q_core, q_y, q_z, rs_send.at[0], rs_recv.at[0], produce_q)
+    kv_sum = ReduceScatter(
+        kv_parts, kv_core, kv_y, kv_z, rs_send.at[1], rs_recv.at[1], produce_kv
+    )
+    query = q_sum.run().astype(jnp.bfloat16)
+    q_all[c, z, y] = query
+    qkv[:, :128] = query
+
+    def consume_q(core, source):
+        if len(kv_sum.first) < NZ:
+            kv_sum.pass_core(len(kv_sum.first))
+        for side in range(2):
+            q_rows[:, columns_of(core, source, side, 128)] = q_all[core, source, side].astype(
+                jnp.float32
+            )
+
+    copies += all_gather(q_all, ag_send.at[2], ag_recv.at[2], consume_q)
+    kv_sum.own()
+    for turn in range(NZ):
+        kv_sum.pass_y(turn)
+    tops[...] = jnp.zeros_like(tops)
+    totals[...] = jnp.zeros_like(totals)
+    owned[...] = jnp.full_like(owned, -1.0)
+
+    def visit(turn, carry):
+        visit_pages(
+            turn, owners, numbers, lengths, slopes, keys, values, page_out, q_rows, tops, totals,
+            owned,
+        )
+        return carry
+
+    arrivals = []
+    for half in range(2):
+        for load in page_loads[half * nturns : (half + 1) * nturns]:
+            load.wait()
+        lax.fori_loop(half * nturns // 2, (half + 1) * nturns // 2, visit, 0)
+        if half == 0:
+            for turn in range(NZ - 1):
+                kv_sum.pass_z(turn)
+        else:
+            write_marks(marks, tops, totals, owned)
+        rows = pl.ds(half * npages, npages)
+        for step in range(1, NSEQ):
+            to = (me + step) % NSEQ
+            n = 3 * (step - 1) + half
+            arrivals.append(
+                send(
+                    page_out.at[to, rows],
+                    got_out.at[me, rows],
+                    ex_send.at[n],
+                    ex_recv.at[n],
+                    to,
+                )
+            )
+            if half == 1:
+                arrivals.append(
+                    send(
+                        marks.at[to], got_marks.at[me], ex_send.at[n + 1], ex_recv.at[n + 1], to
+                    )
+                )
     got_out[me] = page_out[me]
     got_marks[me] = marks[me]
-    for copy in copies:
+    qkv[:, 128:] = kv_sum.collect().astype(jnp.bfloat16)
+    copies += q_sum.copies() + kv_sum.copies() + arrivals
+    for copy in arrivals:
         copy.wait_recv()
     attended[c, z, y] = combine(qkv, slopes, got_out, got_marks)
     contract = (((1,), (1,)), ((), ()))
@@ -751,7 +743,7 @@
         tokens[...].astype(jnp.float32) + (projected.astype(jnp.float32) + pair_out[0, 1].astype(jnp.float32))
     ).astype(jnp.bfloat16)
     hidden_float = hidden_in.astype(jnp.float32)
-    stat_copies = start_stats(hidden_float, stats, stat_send, stat_recv)
+    stat_copies = start_stats(hidden_float, stats, stat_send.at[1], stat_recv.at[1])
     copies += stat_copies
     mean, scale = finish_stats(stat_copies, stats)
     normed = ((hidden_float - mean) * scale * gain[...]).astype(jnp.bfloat16)
@@ -775,8 +767,11 @@
                 preferred_element_type=jnp.float32,
             )
 
-    total, sent = reduce_scatter(parts, from_core, from_y, from_z, rs_send, rs_recv, produce)
-    copies += sent
+    up_sum = ReduceScatter(
+        parts, from_core, from_y, from_z, rs_send.at[2], rs_recv.at[2], produce
+    )
+    total = up_sum.run()
+    copies += up_sum.copies()
     hidden[c, z, y] = (0.5 * total * (1.0 + lax.erf(total * 0.5**0.5))).astype(jnp.bfloat16)
     loads[2].wait()
     copies += all_gather(hidden, ag_send.at[1], ag_recv.at[1], consume_hidden)
@@ -792,52 +787,7 @@
         copy.wait_send()
 
 
-def finish_layer(tokens, qkv, slopes, gain, page_out, marks, w_out, w_up, w_down):
-    rows, local_width = tokens.shape
-    share = w_up.shape[1] // NSEQ
-    vmem = pl.BlockSpec(memory_space=pltpu.VMEM)
-    hbm = pl.BlockSpec(memory_space=pl.ANY)
-    dma = pltpu.SemaphoreType.DMA
-    bf16 = jnp.bfloat16
-    return pl.pallas_call(
-        finish_kernel,
-        out_shape=jax.ShapeDtypeStruct((rows, local_width), bf16),
-        in_specs=[vmem] * 6 + [hbm] * 3,
-        out_specs=vmem,
-        scratch_shapes=[
-            pltpu.VMEM(w_out.shape, bf16),
-            pltpu.VMEM(w_up.shape, bf16),
-            pltpu.VMEM(w_down.shape, bf16),
-            pltpu.VMEM(page_out.shape, bf16),
-            pltpu.VMEM(marks.shape, jnp.float32),
-            pltpu.VMEM((2, NZ, 2, rows, 128), bf16),
-            pltpu.VMEM((2, 2, rows, local_width), bf16),
-            pltpu.VMEM((NSEQ, 16, rows), jnp.float32),
-            pltpu.VMEM((2, NZ, 2, rows, share), bf16),
-            pltpu.VMEM((NZ, 2, rows, share), bf16),
-            pltpu.VMEM((NZ, rows, share), bf16),
-            pltpu.VMEM((NZ - 1, rows, share), bf16),
-            pltpu.VMEM((2, NZ, 2, rows, share), bf16),
-            dma((2 * NSEQ - 2,)),
-            dma((2 * NSEQ - 2,)),
-            dma((2,)),
-            dma((2,)),
-            dma((NSEQ - 1,)),
-            dma((NSEQ - 1,)),
-            dma((COPIES,)),
-            dma((COPIES,)),
-            dma((2, COPIES)),
-            dma((2, COPIES)),
-            dma((3,)),
-        ],
-        compiler_params=pltpu.CompilerParams(
-            collective_id=1, has_side_effects=True, vmem_limit_bytes=VMEM_LIMIT
-        ),
-        name="finish_layer",
-    )(tokens, qkv, slopes, gain, page_out, marks, w_out, w_up, w_down)
-
-
-def on_device_kernels(
+def on_device_kernel(
     tokens,
     lengths,
     page_owner,
@@ -853,14 +803,86 @@
     w_down,
 ):
     nsteps, requests, local_width = tokens.shape
-    rows = tokens.reshape(nsteps * requests, local_width)
-    slopes = alibi_slopes[None, :]
-    q_all, qkv = project(rows, norm1_gain[None, :], jnp.transpose(w_qkv, (1, 0, 2)))
-    page_out, marks = attend_pages(
-        page_owner, page_number, lengths, q_all, slopes, key_pages, value_pages
-    )
-    result = finish_layer(
-        rows, qkv, slopes, norm2_gain[None, :], page_out, marks, w_out, w_up, w_down
+    rows = nsteps * requests
+    npages = key_pages.shape[0]
+    share = w_up.shape[1] // NSEQ
+    by_input = jnp.transpose(w_qkv, (1, 0, 2))
+    vmem = pl.BlockSpec(memory_space=pltpu.VMEM)
+    smem = pl.BlockSpec(memory_space=pltpu.SMEM)
+    hbm = pl.BlockSpec(memory_space=pl.ANY)
+    dma = pltpu.SemaphoreType.DMA
+    bf16 = jnp.bfloat16
+    f32 = jnp.float32
+
+    def sums(width):
+        return [
+            pltpu.VMEM((2, NZ, 2, rows, width), bf16),
+            pltpu.VMEM((NZ, 2, rows, width), bf16),
+            pltpu.VMEM((NZ, rows, width), bf16),
+            pltpu.VMEM((NZ - 1, rows, width), bf16),
+        ]
+
+    result = pl.pallas_call(
+        layer_kernel,
+        out_shape=jax.ShapeDtypeStruct((rows, local_width), bf16),
+        in_specs=[smem] * 3 + [vmem] * 4 + [hbm] * 6,
+        out_specs=vmem,
+        scratch_shapes=[
+            pltpu.VMEM(by_input.shape, bf16),
+            pltpu.VMEM(key_pages.shape, bf16),
+            pltpu.VMEM(value_pages.shape, bf16),
+            pltpu.VMEM(w_out.shape, bf16),
+            pltpu.VMEM(w_up.shape, bf16),
+            pltpu.VMEM(w_down.shape, bf16),
+            *sums(128),
+            *sums(256),
+            pltpu.VMEM((2, NZ, 2, rows, 128), bf16),
+            pltpu.VMEM((rows, 384), bf16),
+            pltpu.VMEM((rows, NSEQ * 128), f32),
+            pltpu.VMEM((2 * NSEQ, 128), f32),
+            pltpu.VMEM((2 * NSEQ, 128), f32),
+            pltpu.VMEM((8, 128), f32),
+            pltpu.VMEM((NSEQ, 2 * npages, 128), bf16),
+            pltpu.VMEM((NSEQ, 4, 128), f32),
+            pltpu.VMEM((NSEQ, 2 * npages, 128), bf16),
+            pltpu.VMEM((NSEQ, 4, 128), f32),
+            pltpu.VMEM((2, NZ, 2, rows, 128), bf16),
+            pltpu.VMEM((2, 2, rows, local_width), bf16),
+            pltpu.VMEM((NSEQ, 2, rows), f32),
+            pltpu.VMEM((NSEQ, 2, rows), f32),
+            *sums(share),
+            pltpu.VMEM((2, NZ, 2, rows, share), bf16),
+            dma((3 * NSEQ - 3,)),
+            dma((3 * NSEQ - 3,)),
+            dma((2,)),
+            dma((2,)),
+            dma((2, NSEQ - 1)),
+            dma((2, NSEQ - 1)),
+            dma((3, COPIES)),
+            dma((3, COPIES)),
+            dma((3, COPIES)),
+            dma((3, COPIES)),
+            dma((4,)),
+            dma((npages // PAGES_STEP, 2)),
+        ],
+        compiler_params=pltpu.CompilerParams(
+            collective_id=0, has_side_effects=True, vmem_limit_bytes=VMEM_LIMIT
+        ),
+        name="layer",
+    )(
+        page_owner,
+        page_number,
+        lengths,
+        tokens.reshape(rows, local_width),
+        alibi_slopes[None, :],
+        norm1_gain[None, :],
+        norm2_gain[None, :],
+        by_input,
+        key_pages,
+        value_pages,
+        w_out,
+        w_up,
+        w_down,
     )
     return result.reshape(tokens.shape)
 
@@ -883,5 +905,5 @@
     )
     fits = mesh.shape["seq"] == NSEQ and mesh.shape["head"] == 2
     return jax.shard_map(
-        on_device_kernels if fits else on_device, mesh=mesh, in_specs=placed, out_specs=P(None, None, "seq"), check_vma=False
-    )
+        on_device_kernel if fits else on_device, mesh=mesh, in_specs=placed, out_specs=P(None, None, "seq"), check_vma=False
+    )

time: 134 us -> 119 us (0.89)
  Pallas kernels: 132 us -> 116 us
    pallas_call x3 -> x1, Pallas kernels: 132 us -> 116 us  [on_device_kernel(): pl.pallas_call(layer_kernel, out_shape=jax.ShapeDtypeStruct((rows, local_...]
where the time goes in v3:
time: 119 us; the launch traced here: 117 us
  Pallas kernels  116 us (97%)
  local copies, waits for them, and re-layouts  1.47 us (1%)
    pallas_call x1, Pallas kernels, on_device_kernel(): pl.pallas_call(layer_kernel, out_shape=jax.ShapeDtypeStruct((rows, local_...  116 us

profile of v3, /device:TPU:31, one launch (start us, length us, event | category | flops | bytes accessed | tf_op | source)
XLA Modules:
  0.0 117.1 jit_solution(15960647940915151019)
XLA Ops:
  0.0 115.7 %layer.1 = bf16[128,256]{1,0:T(8,128)(2,1)} custom-call(s32[32]{0:T(128)} %owners.1, s32[32]{0:T(128)} %numbers.1, s32[64]{0:T(128)} %lengths.1, bf16[128,256]{1,0:T(8,128)(2,1)} %bitcast.8, f32[1,16]{1,0:T(1,128)} %bitcast.11, f32[1,256]{1,0:T(1,128)} %bitcast.9, f32[1,256]{1,0:T(1,128)} %bitcast.10, bf16[3,256,2048]{2,1,0:T(8,128)(2,1)} %bitcast.6, ...), custom_call_target="tpu_custom_call" | custom-call | tf_op jit(solution)/shard_map/layer/pallas_call | solution.py:825
  115.7 1.5 %copy.15 = bf16[2,64,256]{2,1,0:T(8,128)(2,1)} copy(bf16[2,64,256]{2,1,0:T(8,128)(2,1)} %bitcast.7) | data formatting | bytes 131072
